TPU v7x, 256 devices: a whole 4x4x8 slice. The times are simulated.
256 devices in a mesh: row: 4 (over x), col: 8 (over z_lo, core), depth: 8 (over y, z_hi).
Axes of the slice: x: 4, y: 4, z: 8 (z_hi: 2, z_lo: 4; z = z_hi * 4 + z_lo), core: 2. Of those that a mesh axis runs over, the one named last changes fastest.
Arguments:
- factors: bfloat16 [1280, 480, 480], P(('row', 'col', 'depth')), may hold values from -0.15625 to 0.15625
- amplitudes: bfloat16 [528, 3, 480], P('row', None, 'depth'), may hold values from -0.15625 to 0.15625
Outputs:
- ladder: bfloat16 [528, 480, 480], P('row', 'depth', 'col')
All inputs are finite; a program needn't handle non-finite values.
Results may differ from a plain program's by a relative error of at most 0.015.
Values may be sent and summed in bfloat16 or wider, within the bound.
A program may use at most 192 MiB of HBM per device.

v0:
```python
import jax
import jax.numpy as jnp
from jax import lax
from jax.sharding import PartitionSpec as P


def on_device(factors, amplitudes):
    row_count = lax.axis_size("row")
    col_count = lax.axis_size("col")
    depth_count = lax.axis_size("depth")
    q_local, virt_count, _ = factors.shape
    c_width = amplitudes.shape[1]
    left_local = factors[:, :, :c_width].transpose(0, 2, 1)
    left_side = lax.all_gather(left_local, ("row", "col", "depth"), axis=0, tiled=True)
    left_side = left_side.reshape(row_count, col_count, depth_count, q_local, c_width * virt_count)
    left_side = left_side.transpose(0, 2, 1, 3, 4).reshape(-1, c_width, virt_count)
    blocks = lax.all_to_all(
        lax.all_to_all(factors, "col", split_axis=1, concat_axis=0, tiled=True),
        "depth",
        split_axis=2,
        concat_axis=0,
        tiled=True,
    )
    right_side = lax.all_gather(blocks, "row", axis=0, tiled=True)
    aux_count, b_local, d_local = right_side.shape
    right_flat = right_side.reshape(aux_count, b_local * d_local)
    a_count = left_side.shape[2]
    rebuilt = lax.dot_general(
        left_side.reshape(aux_count, c_width * a_count),
        right_flat,
        (((0,), (0,)), ((), ())),
        preferred_element_type=jnp.float32,
    ).astype(jnp.bfloat16)
    rebuilt = (
        rebuilt.reshape(c_width, a_count, b_local, d_local)
        .transpose(0, 3, 1, 2)
        .reshape(c_width * d_local, a_count * b_local)
    )
    pair_count = amplitudes.shape[0]
    product = jnp.dot(
        amplitudes.reshape(pair_count, c_width * d_local),
        rebuilt,
        preferred_element_type=jnp.float32,
    )
    partial_sum = product.reshape(pair_count, a_count, b_local)
    return lax.psum_scatter(
        partial_sum.astype(jnp.bfloat16), "depth", scatter_dimension=1, tiled=True
    )


def solution(mesh):
    in_specs = (P(("row", "col", "depth"), None, None), P("row", None, "depth"))
    out_specs = P("row", "depth", "col")
    return jax.shard_map(
        on_device, mesh=mesh, in_specs=in_specs, out_specs=out_specs, check_vma=False
    )
```

profile of v0, /device:TPU:1, one launch (start us, length us, event | category | flops | bytes accessed | tf_op | source)
XLA Modules:
  0.0 1528.3 jit_solution(6871127304649831332)
XLA Ops:
  6.5 5.2 copy.15
  11.7 7.6 all-to-all-start
  20.3 89.0 %all-to-all-done = bf16[5,480,480]{2,0,1:T(8,128)(2,1)} async-done(((bf16[5,480,480]{2,0,1:T(8,128)(2,1)}), bf16[5,480,480]{2,0,1:T(8,128)(2,1)}, u32[]{:S(2)}, u32[]{:S(2)}) %all-to-all-start) | async-done | bytes 2304032 | tf_op jit(solution)/shard_map/all_to_all | solution.py:18
  112.5 4.8 copy.18
  117.3 10.3 reshape.22
  127.7 60.9 %all_to_all.36 = bf16[8,2,72000]{2,1,0:T(2,128)(2,1)} all-to-all(bf16[8,2,72000]{2,1,0:T(2,128)(2,1)S(1)} %reshape.22), channel_id=1, replica_groups=mesh['row'=4,'col'=8,'depth'=8] {'depth'}, dimensions={0} | all-to-all | bytes 4608000 | tf_op jit(solution)/shard_map/all_to_all | solution.py:17
  188.5 12.7 reshape.23
  201.2 8.7 copy.20
  210.2 553.4 %all-gather.3.cloned.1.call-done = bf16[1280,3,480]{2,1,0:T(4,128)(2,1)} async-done(((bf16[5,3,480]{2,1,0:T(4,128)(2,1)}), bf16[1280,3,480]{2,1,0:T(4,128)(2,1)}) %all-gather.3.cloned.1.call-update) | async-done | bytes 3686416 | tf_op jit(solution)/shard_map/all_gather | solution.py:14
  763.6 13.6 reshape.17
  777.2 6.4 copy.14
  783.6 8.1 reshape_reshape.3
  791.7 170.6 %all-gather.5.cloned.1.call-done = bf16[1280,60,60]{2,0,1:T(8,128)(2,1)} async-done(((bf16[320,60,60]{2,0,1:T(8,128)(2,1)}), bf16[1280,60,60]{2,0,1:T(8,128)(2,1)}) %all-gather.5.cloned.1.call-update) | async-done | bytes 9216016 | tf_op jit(solution)/shard_map/all_gather | solution.py:24
  962.2 19.8 %copy.21 = bf16[1280,60,60]{0,2,1:T(8,128)(2,1)} copy(bf16[1280,60,60]{2,0,1:T(8,128)(2,1)} %all-gather.5.cloned.1.call-done) | data formatting | bytes 18432000 | tf_op jit(solution)/shard_map/all_gather | solution.py:24
  982.0 12.7 reshape.18
  994.7 21.1 %convolution_convert_fusion.1 = bf16[1440,3600]{1,0:T(8,128)(2,1)} fusion(bf16[1280,1440]{1,0:T(8,128)(2,1)} %reshape_reshape.3, bf16[1280,3600]{0,1:T(8,128)(2,1)} %reshape.18), kind=kOutput, calls=%fused_computation.2 | convolution fusion | flops 13276223488 | bytes 23270400 | tf_op jit(solution)/shard_map/dot_general | solution.py:28
  1015.8 15.5 %copy.22 = bf16[1440,3600]{0,1:T(8,128)(2,1)} copy(bf16[1440,3600]{1,0:T(8,128)(2,1)} %convolution_convert_fusion.1) | data formatting | bytes 20736000 | tf_op jit(solution)/shard_map/convert_element_type | solution.py:33
  1031.3 36.7 %reshape.19 = bf16[3,480,60,60]{1,0,3,2:T(4,128)(2,1)} reshape(bf16[1440,3600]{0,1:T(8,128)(2,1)} %copy.22) | data formatting | bytes 20736000 | tf_op jit(solution)/shard_map/reshape | solution.py:35
  1068.0 30.9 %copy.23 = bf16[3,60,480,60]{3,2,1,0:T(8,128)(2,1)} copy(bf16[3,60,480,60]{2,0,1,3:T(4,128)(2,1)} %bitcast.29) | data formatting | bytes 20736000 | tf_op jit(solution)/shard_map/transpose | solution.py:36
  1098.9 41.7 %reshape.20 = bf16[180,28800]{1,0:T(8,128)(2,1)} reshape(bf16[3,60,480,60]{3,2,1,0:T(8,128)(2,1)} %copy.23) | data formatting | bytes 20736000 | tf_op jit(solution)/shard_map/reshape | solution.py:37
  1140.6 9.3 fusion
  1149.9 52.9 %convert_element_type.15 = bf16[132,480,60]{2,1,0:T(8,128)(2,1)} reshape(bf16[132,28800]{1,0:T(8,128)(2,1)} %fusion) | data formatting | bytes 15206400 | tf_op jit(solution)/shard_map/convert_element_type | solution.py:47
  1202.8 28.7 %copy.24 = bf16[132,480,60]{0,2,1:T(8,128)(2,1)} copy(bf16[132,480,60]{2,1,0:T(8,128)(2,1)} %convert_element_type.15) | data formatting | bytes 15206400 | tf_op jit(solution)/shard_map/convert_element_type | solution.py:47
  1231.5 290.3 %reduce-scatter.2.cloned.1.call-done = bf16[132,60,60]{0,2,1:T(8,128)(2,1)} async-done(((bf16[132,480,60]{0,2,1:T(8,128)(2,1)}), bf16[132,60,60]{0,2,1:T(8,128)(2,1)}) %reduce-scatter.2.cloned.1.call-update) | async-done | bytes 950416 | tf_op jit(solution)/shard_map/reduce_scatter | solution.py:46
  (13 shorter events, 4.4 us)
Async XLA Ops:
  6.5 12.9 slice-start
  11.7 97.6 %all-to-all-start = ((bf16[5,480,480]{2,0,1:T(8,128)(2,1)}), bf16[5,480,480]{2,0,1:T(8,128)(2,1)}, u32[]{:S(2)}, u32[]{:S(2)}) async-start(bf16[5,480,480]{2,0,1:T(8,128)(2,1)} %copy.15), calls=%async_computation | async-start | bytes 7864320 | tf_op jit(solution)/shard_map/all_to_all | solution.py:18
  19.4 744.2 %all-gather.3.cloned.1.call-start = ((), (), s32[]{:S(2)}) async-start(), calls=%async_computation.3 | async-start | bytes 5263360 | tf_op jit(solution)/shard_map/all_gather | solution.py:14
  20.3 941.9 %all-gather.5.cloned.1.call-start = ((), (), s32[]{:S(2)}) async-start(), calls=%async_computation.4 | async-start | bytes 24576000 | tf_op jit(solution)/shard_map/all_gather | solution.py:24
  188.5 21.6 %copy-start = (bf16[132,3,60]{0,2,1:T(8,128)(2,1)S(1)}, bf16[132,3,60]{0,2,1:T(8,128)(2,1)}, u32[]{:S(2)}) copy-start(bf16[132,3,60]{0,2,1:T(8,128)(2,1)} %param.3) | copy-start | bytes 142564
  209.9 1311.9 %reduce-scatter.2.cloned.1.call-start = ((), (), s32[]{:S(2)}) async-start(), calls=%async_computation.5 | async-start | bytes 17694720 | tf_op jit(solution)/shard_map/reduce_scatter | solution.py:46
Sparse Core Ops, SparseCore 0:
  22.1 741.4 all-gather.2
  765.4 196.7 all-gather.4
  1231.6 290.1 reduce-scatter.1
where the time goes:
time: 1530 us
  waiting for transfers between devices  1100 us (72%)
  local copies, waits for them, and re-layouts  313 us (20%)
  blocking collectives  60.9 us (4%)
  matrix products  30.4 us (2%)
    all_gather x1, waiting for transfers between devices, on_device(): lax.all_gather(left_local, ('row', 'col', 'depth'), axis=0, tiled=True)  553 us
    reduce_scatter x1, waiting for transfers between devices, on_device(): lax.psum_scatter(partial_sum.astype(jnp.bfloat16), 'depth', scatter_dimen...  290 us
    all_gather x1, waiting for transfers between devices, on_device(): right_side = lax.all_gather(blocks, 'row', axis=0, tiled=True)  171 us
    all_to_all x1, waiting for transfers between devices, on_device(): lax.all_to_all(factors, 'col', split_axis=1, concat_axis=0, tiled=True)  89 us
    convert_element_type x2, local copies, waits for them, and re-layouts, on_device(): partial_sum.astype(jnp.bfloat16)  81.5 us
    all_to_all x1, blocking collectives, on_device(): lax.all_to_all(lax.all_to_all(factors, 'col', split_axis=1, concat_axis=0...  60.9 us
    reshape x1, local copies, waits for them, and re-layouts, on_device(): rebuilt = rebuilt.reshape(c_width, a_count, b_local, d_local).transpose(0...  41.7 us
    reshape x1, local copies, waits for them, and re-layouts, on_device(): rebuilt.reshape(c_width, a_count, b_local, d_local).transpose(0, 3, 1, 2)  36.7 us
  transfers between devices with their start and end apart: 4, of which 4 were waited for; matrix products, arithmetic and copies ran while one was open for 4% of the time, Pallas kernels for 0%

commit v1 on v0

v1 whole, which is shorter than its diff:
```python
import jax
import jax.numpy as jnp
from jax import lax
from jax.experimental import pallas as pl
from jax.experimental.pallas import tpu as pltpu
from jax.sharding import PartitionSpec as P

NV = 480
BLOCKS = 8
BLOCK = 60
PAD = 64
NVP = BLOCKS * PAD
LANE = 128
TILES = NVP // LANE
Q_LOCAL = 5
DEVICES = 256
NAUX = Q_LOCAL * DEVICES
CW = 3
ROWS_X = 132
GROUPS = 17
ROWS_P = GROUPS * 8
PAIR_ROWS = 4 * ROWS_P
B_PAIRS = 240
ACTIVE = 30
KDIM = CW * NVP
BF16 = jnp.bfloat16
F32 = jnp.float32
MIB = 1 << 20


def ones_where(mask):
    return jnp.where(mask, 1.0, 0.0).astype(BF16)


def iotas(rows, columns):
    shape = (rows, columns)
    return lax.broadcasted_iota(jnp.int32, shape, 0), lax.broadcasted_iota(jnp.int32, shape, 1)


def dot(left, right):
    return jnp.dot(left, right, preferred_element_type=F32)


def dot_nt(left, right):
    return lax.dot_general(left, right, (((1,), (1,)), ((), ())), preferred_element_type=F32)


def spread_matrix():
    row, column = iotas(NV, NVP)
    within = column & (PAD - 1)
    return ones_where((row == (column >> 6) * BLOCK + within) & (within < BLOCK))


def prep_kernel(f_ref, t_ref, send_ref, left_ref, t_out_ref):
    spread = spread_matrix()
    out_row, in_row = iotas(LANE, LANE)
    gather_rows = ones_where(
        in_row == (out_row & 3) * 32 + (out_row >> 3) * 2 + ((out_row >> 2) & 1)
    )
    row, column = iotas(16, NV)
    pick = ones_where((row == column) & (row < CW))
    left_tiles = []
    for q in range(Q_LOCAL):
        wide = dot(f_ref[q], spread).astype(BF16)
        for chunk in range(NV // 32):
            rows = wide[32 * chunk : 32 * chunk + 32]
            stacked = jnp.concatenate(
                [rows[:, LANE * t : LANE * (t + 1)] for t in range(TILES)], axis=0
            )
            moved = dot(gather_rows, stacked).reshape(16, 8, LANE)
            send_ref[16 * chunk : 16 * chunk + 16, q] = moved.astype(BF16)
        picked = dot(dot_nt(pick, f_ref[q]).astype(BF16), spread).astype(BF16)
        left_tiles += [picked[:, LANE * t : LANE * (t + 1)] for t in range(TILES)]
    out_row, in_row = iotas(64, 64 * Q_LOCAL)
    place = ones_where(
        (out_row == (in_row >> 6) * 12 + (in_row & 15) * 4 + ((in_row >> 4) & 3))
        & ((in_row & 15) < CW)
    )
    left_ref[...] = dot(place, jnp.concatenate(left_tiles, axis=0)).reshape(8, 8, LANE).astype(BF16)
    z_hi = lax.rem(lax.axis_index("depth"), 2)
    row, column = iotas(BLOCK, LANE)
    low = ones_where(row == column)
    high = ones_where(row + PAD == column)
    either = ones_where(row + PAD * z_hi == column)
    t_out_ref[0] = (dot(t_ref[0], low) + dot(t_ref[1], high)).astype(BF16)
    t_out_ref[1] = dot(t_ref[2], either).astype(BF16)


def place_of(row, col, depth):
    return row, depth // 2, (depth % 2) * 4 + col // 2, col % 2


def mesh_id(x, y, z, core):
    return {"row": x, "col": (z % 4) * 2 + core, "depth": y * 2 + z // 4}


def exchange_kernel(
    send_ref, left_in, t_in, right_ref, left_ref, t_ref,
    a2a_send, a2a_recv, l_send, l_recv, t_send, t_recv, own_sem,
):
    x, y, z, core = place_of(lax.axis_index("row"), lax.axis_index("col"), lax.axis_index("depth"))
    z_hi = z // 4
    me = core * 128 + x * 32 + y * 8 + z
    active = x * 8 + y * 2 + z_hi < ACTIVE

    def remote(src, dst, send, recv, to):
        return pltpu.make_async_remote_copy(
            src_ref=src, dst_ref=dst, send_sem=send, recv_sem=recv,
            device_id=mesh_id(*to), device_id_type=pl.DeviceIdType.MESH,
        )

    def wait(ref, sem):
        pltpu.make_async_copy(ref, ref, sem).wait()

    own_left = pltpu.make_async_copy(left_in, left_ref.at[:, core, x, y, z], own_sem.at[0])
    own_left.start()
    own_t = pltpu.make_async_copy(t_in.at[core], t_ref.at[core, x, y, z_hi], own_sem.at[1])
    own_t.start()
    remote(
        t_in.at[core], t_ref.at[core, x, y, z_hi], t_send.at[0], t_recv.at[0], (x, y, 7 - z, core)
    ).start()

    @pl.loop(1, 8)
    def _(step):
        remote(
            left_in, left_ref.at[:, core, x, y, z], l_send.at[0], l_recv.at[0],
            (x, y, (z + step) % 8, core),
        ).start()

    def send_right(first, last):
        @pl.loop(first, last)
        def _(step):
            to_z = (z + step) % 8
            to_core = (core + step // 8) % 2
            to_y = (y + step // 16) % 4
            to_x = (x + step // 64) % 4
            group = to_x * 8 + to_y * 2 + to_z // 4
            pair = ACTIVE * (((to_z + 2) % 4) * 2 + to_core) + group

            @pl.when(group < ACTIVE)
            def _():
                remote(
                    send_ref.at[pair], right_ref.at[:, me], a2a_send, a2a_recv,
                    (to_x, to_y, to_z, to_core),
                ).start()

    @pl.when(active)
    def _():
        pair = ACTIVE * (((z + 2) % 4) * 2 + core) + x * 8 + y * 2 + z_hi
        pltpu.make_async_copy(send_ref.at[pair], right_ref.at[:, me], own_sem.at[2]).start()

    send_right(1, 64)

    own_left.wait()
    wait(left_ref.at[:, 0, 0, 0, 0:7], l_recv.at[0])
    own_t.wait()
    wait(t_ref.at[0, 0, 0, 0], t_recv.at[0])

    @pl.loop(1, 4)
    def _(step):
        block = left_ref.at[0:4, core, x, y]
        remote(block, block, l_send.at[1], l_recv.at[1], (x, (y + step) % 4, z, core)).start()
        block = left_ref.at[4:8, core, x, y]
        remote(block, block, l_send.at[2], l_recv.at[2], ((x + step) % 4, y, z, core)).start()
        block = t_ref.at[core, x, y]
        to = ((x + step * core) % 4, (y + step * (1 - core)) % 4, z, core)
        remote(block, block, t_send.at[1], t_recv.at[1], to).start()

    send_right(64, 128)

    wait(left_ref.at[0:4, 0, 0, 0:3], l_recv.at[1])
    wait(left_ref.at[0:4, 0, 0, 0:3], l_recv.at[2])
    wait(t_ref.at[0, 0, 0:3], t_recv.at[1])

    @pl.loop(1, 4)
    def _(step):
        block = left_ref.at[0:4, core, x]
        remote(block, block, l_send.at[3], l_recv.at[3], ((x + step) % 4, y, z, core)).start()
        block = left_ref.at[4:8, core, :, y]
        remote(block, block, l_send.at[4], l_recv.at[4], (x, (y + step) % 4, z, core)).start()

        @pl.when(core == 0)
        def _():
            block = t_ref.at[0, x]
            remote(block, block, t_send.at[2], t_recv.at[2], ((x + step) % 4, y, z, core)).start()

        @pl.when(core == 1)
        def _():
            block = t_ref.at[1, :, y]
            remote(block, block, t_send.at[2], t_recv.at[2], (x, (y + step) % 4, z, core)).start()

    send_right(128, 256)

    wait(left_ref.at[0:4, 0, 0:3], l_recv.at[3])
    wait(left_ref.at[0:4, 0, 0:3], l_recv.at[4])
    sibling = (x, y, z, 1 - core)
    block = left_ref.at[:, core]
    swap_left = remote(block, block, l_send.at[5], l_recv.at[5], sibling)
    swap_left.start()
    wait(t_ref.at[0, 0:3], t_recv.at[2])
    block = t_ref.at[core]
    swap_t = remote(block, block, t_send.at[3], t_recv.at[3], sibling)
    swap_t.start()

    swap_left.wait()
    swap_t.wait()
    wait(left_ref.at[:, 0, 0, 0, 0:7], l_send.at[0])
    wait(left_ref.at[0:4, 0, 0, 0:3], l_send.at[1])
    wait(left_ref.at[0:4, 0, 0, 0:3], l_send.at[2])
    wait(left_ref.at[0:4, 0, 0:3], l_send.at[3])
    wait(left_ref.at[0:4, 0, 0:3], l_send.at[4])
    wait(t_ref.at[0, 0, 0, 0], t_send.at[0])
    wait(t_ref.at[0, 0, 0:3], t_send.at[1])
    wait(t_ref.at[0, 0:3], t_send.at[2])

    @pl.when(active)
    def _():
        wait(send_ref.at[0 : B_PAIRS - 1], a2a_send)
        wait(right_ref.at[:, 0], own_sem.at[2])
        wait(right_ref.at[:, 0 : DEVICES - 1], a2a_recv)

    @pl.when(jnp.logical_not(active))
    def _():
        wait(send_ref, a2a_send)


def compute_kernel(right_ref, left_ref, t_ref, out_ref, left2, right_n, right_t, mid, t_cat, total):
    out_row, in_row = iotas(256, 256)
    sort_rows = ones_where(in_row == ((out_row & 31) << 3) + (out_row >> 5))
    row, column = iotas(LANE, LANE)
    identity = ones_where(row == column)

    for q in range(Q_LOCAL):
        for chunk in range(8):
            block = right_ref[q, 32 * chunk : 32 * chunk + 32].astype(F32).reshape(256, LANE)
            moved = dot(sort_rows, block.astype(BF16)).astype(BF16)
            for r in range(8):
                base = 256 * q + 32 * chunk
                right_n[r, base : base + 32, :] = moved[32 * r : 32 * r + 32]
        for r in range(8):
            block = right_n[r, 256 * q : 256 * q + 256, :]
            right_t[LANE * r : LANE * r + LANE, 256 * q : 256 * q + 256] = dot_nt(
                identity, block
            ).astype(BF16)
    for group in range(8):
        for chunk in range(8):
            block = left_ref[group, 32 * chunk : 32 * chunk + 32].astype(F32).reshape(256, LANE)
            moved = dot(sort_rows, block.astype(BF16)).astype(BF16)
            for r in range(8):
                q, tile = divmod(8 * group + r, 12)
                if q < Q_LOCAL:
                    base = 256 * q + 32 * chunk
                    left2[base : base + 32, LANE * tile : LANE * tile + LANE] = moved[
                        32 * r : 32 * r + 32
                    ]
    for m in range(4):
        which, half = divmod(m, 2)
        for c in range(CW):
            rebuilt = dot(
                right_t[256 * m : 256 * m + 256, :], left2[:, NVP * c : NVP * c + NVP]
            ).astype(BF16)
            if c < 2:
                for k in range(4):
                    base = (4 * half + k) * LANE + PAD * c
                    mid[which, base : base + PAD, :] = rebuilt[PAD * k : PAD * k + PAD]
            else:
                base = 2 * NVP + 256 * half
                mid[which, base : base + 256, :] = rebuilt
    for x in range(4):
        rows = slice(ROWS_P * x, ROWS_P * x + ROWS_P)
        for k in range(BLOCKS):
            t_cat[rows, LANE * k : LANE * k + LANE] = t_ref[0, x, k].astype(F32)
        for y in range(4):
            base = 2 * NVP + LANE * y
            t_cat[rows, base : base + LANE] = t_ref[1, x, 2 * y].astype(F32) + t_ref[
                1, x, 2 * y + 1
            ].astype(F32)
    t_all = t_cat[...].astype(BF16)
    for which in range(2):
        total[which] = dot(t_all, mid[which])
    first_half = lax.broadcasted_iota(jnp.int32, (ROWS_P, LANE), 1) < PAD
    for x in range(4):
        rows = slice(ROWS_P * x, ROWS_P * x + ROWS_P)
        for y in range(4):
            lanes = slice(LANE * y, LANE * y + LANE)
            one, two = total[0, rows, lanes], total[1, rows, lanes]
            even = jnp.where(first_half, one, pltpu.roll(two, PAD, 1))
            odd = jnp.where(first_half, pltpu.roll(one, PAD, 1), two)
            out_ref[x, 2 * y] = even.reshape(GROUPS, 8, LANE).astype(BF16)
            out_ref[x, 2 * y + 1] = odd.reshape(GROUPS, 8, LANE).astype(BF16)


def scatter_kernel(in_ref, out_ref, send_sem, recv_sem):
    x, y, z, core = place_of(lax.axis_index("row"), lax.axis_index("col"), lax.axis_index("depth"))
    group = x * 8 + y * 2 + z // 4

    @pl.when(group < ACTIVE)
    def _():
        @pl.loop(0, 32)
        def _(step):
            to_z = (z + 2 + 4 * (step % 2)) % 8
            to_y = (y + step // 2) % 4
            to_x = (x + step // 8) % 4
            pltpu.make_async_remote_copy(
                src_ref=in_ref.at[to_x, to_y * 2 + to_z // 4],
                dst_ref=out_ref.at[group],
                send_sem=send_sem,
                recv_sem=recv_sem,
                device_id=mesh_id(to_x, to_y, to_z, core),
                device_id_type=pl.DeviceIdType.MESH,
            ).start()

    block = out_ref.at[0:ACTIVE]
    pltpu.make_async_copy(block, block, recv_sem).wait()

    @pl.when(group < ACTIVE)
    def _():
        pltpu.make_async_copy(in_ref, in_ref, send_sem).wait()


def finish_kernel(in_ref, out_ref, turned, result):
    row, column = iotas(LANE, LANE)
    identity = ones_where(row == column)
    row, column = iotas(512, 1024)
    place = ones_where(
        ((column >> 7) == (row & 7)) & ((column & 127) == 2 * ((row >> 3) & 31) + (row >> 8))
    )
    for group in range(GROUPS):
        block = in_ref[0:ACTIVE, group].astype(F32).reshape(8 * ACTIVE, LANE)
        block = jnp.concatenate([block, jnp.zeros((16, LANE), F32)], axis=0).astype(BF16)
        flipped = dot_nt(identity, block).astype(BF16)
        turned[PAD * group : PAD * group + PAD, 0:256] = flipped[0:PAD]
        turned[PAD * group : PAD * group + PAD, 256:512] = flipped[PAD:LANE]
    result[...] = dot(turned[...], place)
    for pair in range(ROWS_X):
        group, within = divmod(pair, 8)
        block = result[PAD * group : PAD * group + PAD, LANE * within : LANE * within + LANE]
        out_ref[pair] = block.astype(BF16)[0:BLOCK, 0:BLOCK]


def vmem(count):
    return [pl.BlockSpec(memory_space=pltpu.VMEM)] * count


def anywhere(count):
    return [pl.BlockSpec(memory_space=pl.ANY)] * count


def shape(*sizes):
    return jax.ShapeDtypeStruct(sizes, BF16)


def prepare(factors, amplitudes):
    t_local = jnp.pad(amplitudes.transpose(1, 0, 2), ((0, 0), (0, ROWS_P - ROWS_X), (0, 0)))
    return pl.pallas_call(
        prep_kernel,
        out_shape=(shape(B_PAIRS, Q_LOCAL, 8, LANE), shape(8, 8, LANE), shape(2, ROWS_P, LANE)),
        in_specs=vmem(2),
        out_specs=tuple(vmem(3)),
        compiler_params=pltpu.CompilerParams(vmem_limit_bytes=40 * MIB),
        name="prepare",
    )(factors, t_local)


def exchange(send, left_own, t_own):
    dma = pltpu.SemaphoreType.DMA
    return pl.pallas_call(
        exchange_kernel,
        out_shape=(
            shape(Q_LOCAL, DEVICES, 8, LANE),
            shape(8, 2, 4, 4, 8, 8, LANE),
            shape(2, 4, 4, 2, ROWS_P, LANE),
        ),
        in_specs=anywhere(3),
        out_specs=tuple(anywhere(3)),
        scratch_shapes=[dma, dma, dma((6,)), dma((6,)), dma((4,)), dma((4,)), dma((3,))],
        compiler_params=pltpu.CompilerParams(has_side_effects=True),
        name="exchange",
    )(send, left_own, t_own)


def compute(right, left, t_full):
    return pl.pallas_call(
        compute_kernel,
        out_shape=shape(4, BLOCKS, GROUPS, 8, LANE),
        in_specs=vmem(3),
        out_specs=vmem(1)[0],
        scratch_shapes=[
            pltpu.VMEM((NAUX, KDIM), BF16),
            pltpu.VMEM((8, NAUX, LANE), BF16),
            pltpu.VMEM((2 * NVP, NAUX), BF16),
            pltpu.VMEM((2, KDIM, NVP), BF16),
            pltpu.VMEM((PAIR_ROWS, KDIM), F32),
            pltpu.VMEM((2, PAIR_ROWS, NVP), F32),
        ],
        compiler_params=pltpu.CompilerParams(vmem_limit_bytes=56 * MIB),
        name="compute",
    )(
        right,
        left.reshape(8, DEVICES, 8, LANE),
        t_full.reshape(2, 4, BLOCKS, ROWS_P, LANE),
    )


def scatter(blocks):
    dma = pltpu.SemaphoreType.DMA
    return pl.pallas_call(
        scatter_kernel,
        out_shape=shape(32, GROUPS, 8, LANE),
        in_specs=anywhere(1),
        out_specs=anywhere(1)[0],
        scratch_shapes=[dma, dma],
        compiler_params=pltpu.CompilerParams(has_side_effects=True),
        name="scatter",
    )(blocks)


def finish(blocks):
    return pl.pallas_call(
        finish_kernel,
        out_shape=shape(ROWS_X, BLOCK, BLOCK),
        in_specs=vmem(1),
        out_specs=vmem(1)[0],
        scratch_shapes=[
            pltpu.VMEM((PAD * GROUPS, 512), BF16),
            pltpu.VMEM((PAD * GROUPS, 1024), F32),
        ],
        compiler_params=pltpu.CompilerParams(vmem_limit_bytes=40 * MIB),
        name="finish",
    )(blocks)


def on_device(factors, amplitudes):
    return finish(scatter(compute(*exchange(*prepare(factors, amplitudes)))))


def solution(mesh):
    in_specs = (P(("row", "col", "depth"), None, None), P("row", None, "depth"))
    out_specs = P("row", "depth", "col")
    return jax.shard_map(
        on_device, mesh=mesh, in_specs=in_specs, out_specs=out_specs, check_vma=False
    )
```

time: 1530 us -> 160 us (0.10)
  waiting for transfers between devices: 1100 us -> 0 us
  local copies, waits for them, and re-layouts: 313 us -> 10.1 us
  Pallas kernels: 0 us -> 150 us
  blocking collectives: 60.9 us -> 0 us
  matrix products: 30.4 us -> 0 us
    all_gather x2 -> x0, waiting for transfers between devices: 724 us -> none  [the longest x1 553 us: on_device(): lax.all_gather(left_local, ('row', 'col', 'depth'), axis=0, tiled=True)]
    reduce_scatter x1 -> x0, waiting for transfers between devices: 290 us -> none  [on_device(): lax.psum_scatter(partial_sum.astype(jnp.bfloat16), 'depth', scatter_dimen...]
    pallas_call x0 -> x5, Pallas kernels: none -> 150 us  [the longest x1 81.9 us: exchange(): pl.pallas_call(exchange_kernel, out_shape=(shape(Q_LOCAL, DEVICES, 8, LAN...]
    reshape x5 -> x0, local copies, waits for them, and re-layouts: 105 us -> none  [the longest x1 41.7 us: on_device(): rebuilt = rebuilt.reshape(c_width, a_count, b_local, d_local).transpose(0...]
    convert_element_type x3 -> x0, local copies, waits for them, and re-layouts: 97 us -> none  [the longest x2 81.5 us: on_device(): partial_sum.astype(jnp.bfloat16)]
    all_to_all x1 -> x0, waiting for transfers between devices: 89 us -> none  [on_device(): lax.all_to_all(factors, 'col', split_axis=1, concat_axis=0, tiled=True)]
    all_to_all x1 -> x0, blocking collectives: 60.9 us -> none  [on_device(): lax.all_to_all(lax.all_to_all(factors, 'col', split_axis=1, concat_axis=0...]
    transpose x2 -> x0, local copies, waits for them, and re-layouts: 37.3 us -> none  [the longest x1 30.9 us: on_device(): rebuilt = rebuilt.reshape(c_width, a_count, b_local, d_local).transpose(0...]
  transfers between devices with their start and end apart: 4 -> 0, of which waited for: 4 -> 0; matrix products, arithmetic and copies ran while one was open for 4% -> 0% of each run, Pallas kernels for 0% -> 0%
where the time goes in v1:
time: 160 us
  Pallas kernels  150 us (94%)
  local copies, waits for them, and re-layouts  10.1 us (6%)
    pallas_call x1, Pallas kernels, exchange(): pl.pallas_call(exchange_kernel, out_shape=(shape(Q_LOCAL, DEVICES, 8, LAN...  81.9 us
    pallas_call x1, Pallas kernels, scatter(): pl.pallas_call(scatter_kernel, out_shape=shape(32, GROUPS, 8, LANE), in_s...  46.5 us
    pallas_call x1, Pallas kernels, compute(): pl.pallas_call(compute_kernel, out_shape=shape(4, BLOCKS, GROUPS, 8, LANE...  15.5 us
    unnamed x11, local copies, waits for them, and re-layouts  6.69 us
    pallas_call x1, Pallas kernels, prepare(): pl.pallas_call(prep_kernel, out_shape=(shape(B_PAIRS, Q_LOCAL, 8, LANE),...  3.94 us
    pallas_call x1, local copies, waits for them, and re-layouts, finish(): pl.pallas_call(finish_kernel, out_shape=shape(ROWS_X, BLOCK, BLOCK), in_s...  3.38 us

profile of v1, /device:TPU:1, one launch (start us, length us, event | category | flops | bytes accessed | tf_op | source)
XLA Modules:
  0.0 160.0 jit_solution(7599909723798870193)
XLA Ops:
  0.0 1.1 copy.3
  1.1 0.0 copy-start.2
  1.1 1.7 %copy-done.2 = bf16[5,480,480]{2,1,0:T(8,128)(2,1)S(1)} copy-done((bf16[5,480,480]{2,1,0:T(8,128)(2,1)S(1)}, bf16[5,480,480]{2,1,0:T(8,128)(2,1)}, u32[]{:S(2)}) %copy-start.2) | copy-done | bytes 2304024
  2.8 3.9 %prepare.1 = (bf16[240,5,8,128]{3,2,1,0:T(8,128)(2,1)S(1)}, bf16[8,8,128]{2,1,0:T(8,128)(2,1)S(1)}, bf16[2,136,128]{2,1,0:T(8,128)(2,1)S(1)}) custom-call(bf16[5,480,480]{2,1,0:T(8,128)(2,1)S(1)} %copy-done.2, bf16[3,136,60]{2,1,0:T(8,128)(2,1)S(1)} %pad.4.t_ref), custom_call_target="tpu_custom_call" | custom-call | tf_op jit(solution)/shard_map/prepare/pallas_call | solution.py:355
  6.7 0.0 copy-start.1
  6.8 1.5 copy-done.1
  8.2 0.0 copy-start.3
  8.2 0.6 copy-done.3
  8.9 0.0 copy-start.4
  8.9 0.6 copy-done.4
  9.4 81.9 %exchange.1 = (bf16[5,256,8,128]{3,2,1,0:T(8,128)(2,1)}, bf16[8,2,4,4,8,8,128]{6,5,4,3,2,1,0:T(8,128)(2,1)}, bf16[2,4,4,2,136,128]{5,4,3,2,1,0:T(8,128)(2,1)}) custom-call(bf16[240,5,8,128]{3,2,1,0:T(8,128)(2,1)} %copy-done.1, bf16[8,8,128]{2,1,0:T(8,128)(2,1)} %copy-done.4, bf16[2,136,128]{2,1,0:T(8,128)(2,1)} %copy-done.3), custom_call_target="tpu_custom_call" | custom-call | tf_op jit(solution)/shard_map/exchange/pallas_call | solution.py:367
  91.3 15.5 %compute.1.in_ref = bf16[4,8,17,8,128]{4,3,2,1,0:T(8,128)(2,1)} custom-call(bf16[5,256,8,128]{3,2,1,0:T(8,128)(2,1)} %get-tuple-element.14.right_ref, bf16[8,256,8,128]{3,2,1,0:T(8,128)(2,1)} %bitcast.3, bf16[2,4,8,136,128]{4,3,2,1,0:T(8,128)(2,1)} %bitcast.4), custom_call_target="tpu_custom_call" | custom-call | tf_op jit(solution)/shard_map/compute/pallas_call | solution.py:383
  106.8 46.5 %scatter.1.in_ref = bf16[32,17,8,128]{3,2,1,0:T(8,128)(2,1)} custom-call(bf16[4,8,17,8,128]{4,3,2,1,0:T(8,128)(2,1)} %compute.1.in_ref), custom_call_target="tpu_custom_call" | custom-call | tf_op jit(solution)/shard_map/scatter/pallas_call | solution.py:407
  153.3 0.0 copy-start
  153.4 1.2 copy-done
  154.6 2.0 %finish.1 = bf16[132,60,60]{2,1,0:T(8,128)(2,1)S(1)} custom-call(bf16[32,17,8,128]{3,2,1,0:T(8,128)(2,1)S(1)} %copy-done), custom_call_target="tpu_custom_call" | custom-call | tf_op jit(solution)/shard_map/finish/pallas_call | solution.py:419
  156.6 3.4 %copy.4 = bf16[132,60,60]{0,2,1:T(8,128)(2,1)} copy(bf16[132,60,60]{2,1,0:T(8,128)(2,1)S(1)} %finish.1) | data formatting | bytes 1900800 | tf_op jit(solution)/shard_map/finish/pallas_call | solution.py:419
  (1 shorter events, 0.0 us)
Async XLA Ops:
  1.1 1.7 %copy-start.2 = (bf16[5,480,480]{2,1,0:T(8,128)(2,1)S(1)}, bf16[5,480,480]{2,1,0:T(8,128)(2,1)}, u32[]{:S(2)}) copy-start(bf16[5,480,480]{2,1,0:T(8,128)(2,1)} %f_ref.1) | copy-start | bytes 6912004
  6.7 1.5 copy-start.1
  8.2 0.6 copy-start.3
  8.9 0.6 copy-start.4
  153.3 1.2 copy-start

commit v2 on v1

v2 whole, which is shorter than its diff:
```python
import jax
import jax.numpy as jnp
from jax import lax
from jax.experimental import pallas as pl
from jax.experimental.pallas import tpu as pltpu
from jax.sharding import PartitionSpec as P

NV = 480
BLOCKS = 8
BLOCK = 60
PAD = 64
NVP = BLOCKS * PAD
LANE = 128
TILES = NVP // LANE
Q_LOCAL = 5
DEVICES = 256
NAUX = Q_LOCAL * DEVICES
CW = 3
ROWS_X = 132
GROUPS = 17
ROWS_P = GROUPS * 8
B_PAIRS = 240
ACTIVE = 30
KDIM = CW * NVP
LEFT_ROWS = Q_LOCAL * CW * TILES
BF16 = jnp.bfloat16
F32 = jnp.float32
MIB = 1 << 20


def ones_where(mask):
    return jnp.where(mask, 1.0, 0.0).astype(BF16)


def iotas(rows, columns):
    shape = (rows, columns)
    return lax.broadcasted_iota(jnp.int32, shape, 0), lax.broadcasted_iota(jnp.int32, shape, 1)


def dot(left, right):
    return jnp.dot(left, right, preferred_element_type=F32)


def dot_nt(left, right):
    return lax.dot_general(left, right, (((1,), (1,)), ((), ())), preferred_element_type=F32)


def spread_matrix():
    row, column = iotas(NV, NVP)
    within = column & (PAD - 1)
    return ones_where((row == (column >> 6) * BLOCK + within) & (within < BLOCK))


def prep_kernel(f_ref, t_ref, send_ref, left_ref, t_out_ref):
    spread = spread_matrix()
    out_row, in_row = iotas(LANE, LANE)
    gather_rows = ones_where(
        in_row == (out_row & 3) * 32 + (out_row >> 3) * 2 + ((out_row >> 2) & 1)
    )
    row, column = iotas(16, NV)
    pick = ones_where((row == column) & (row < CW))
    left_tiles = []
    for q in range(Q_LOCAL):
        wide = dot(f_ref[q], spread).astype(BF16)
        for chunk in range(NV // 32):
            rows = wide[32 * chunk : 32 * chunk + 32]
            stacked = jnp.concatenate(
                [rows[:, LANE * t : LANE * (t + 1)] for t in range(TILES)], axis=0
            )
            moved = dot(gather_rows, stacked).reshape(16, 8, LANE)
            send_ref[16 * chunk : 16 * chunk + 16, q] = moved.astype(BF16)
        picked = dot(dot_nt(pick, f_ref[q]).astype(BF16), spread).astype(BF16)
        left_tiles += [picked[:, LANE * t : LANE * (t + 1)] for t in range(TILES)]
    out_row, in_row = iotas(64, 64 * Q_LOCAL)
    place = ones_where(
        (out_row == (in_row >> 6) * 12 + (in_row & 15) * 4 + ((in_row >> 4) & 3))
        & ((in_row & 15) < CW)
    )
    left_ref[...] = dot(place, jnp.concatenate(left_tiles, axis=0)).reshape(8, 8, LANE).astype(BF16)
    z_hi = lax.rem(lax.axis_index("depth"), 2)
    row, column = iotas(BLOCK, LANE)
    low = ones_where(row == column)
    high = ones_where(row + PAD == column)
    either = ones_where(row + PAD * z_hi == column)
    both = dot(t_ref[0], low) + dot(t_ref[1], high)
    t_out_ref[0] = both.reshape(GROUPS, 8, LANE).astype(BF16)
    t_out_ref[1] = dot(t_ref[2], either).reshape(GROUPS, 8, LANE).astype(BF16)


def place_of(row, col, depth):
    return row, depth // 2, (depth % 2) * 4 + col // 2, col % 2


def mesh_id(x, y, z, core):
    return {"row": x, "col": (z % 4) * 2 + core, "depth": y * 2 + z // 4}


def wait_bytes(ref, sem):
    pltpu.make_async_copy(ref, ref, sem).wait()


def exchange_kernel(
    send_ref, left_in, t_in, right_ref, left_ref, t_ref,
    staged, bundle, a2a_send, a2a_recv, l_send, l_recv, t_send, t_recv, own_sem,
):
    x, y, z, core = place_of(lax.axis_index("row"), lax.axis_index("col"), lax.axis_index("depth"))
    z_hi = z // 4
    me = core * 128 + x * 32 + y * 8 + z
    active = x * 8 + y * 2 + z_hi < ACTIVE
    half = LEFT_ROWS // 2

    def remote(src, dst, send, recv, to):
        return pltpu.make_async_remote_copy(
            src_ref=src, dst_ref=dst, send_sem=send, recv_sem=recv,
            device_id=mesh_id(*to), device_id_type=pl.DeviceIdType.MESH,
        )

    own_left = pltpu.make_async_copy(left_in, staged.at[z], own_sem.at[0])
    own_left.start()
    own_t = pltpu.make_async_copy(t_in.at[core], t_ref.at[core, y, z_hi, x], own_sem.at[1])
    own_t.start()
    remote(
        t_in.at[core], t_ref.at[core, y, z_hi, x], t_send.at[0], t_recv.at[0], (x, y, 7 - z, core)
    ).start()

    @pl.loop(1, 8)
    def _(step):
        remote(
            left_in, staged.at[z], l_send.at[0], l_recv.at[0], (x, y, (z + step) % 8, core)
        ).start()

    def send_right(first, last):
        @pl.loop(first, last)
        def _(step):
            to_z = (z + step) % 8
            to_core = (core + step // 8) % 2
            to_y = (y + step // 16) % 4
            to_x = (x + step // 64) % 4
            group = to_x * 8 + to_y * 2 + to_z // 4
            pair = ACTIVE * (((to_z + 2) % 4) * 2 + to_core) + group

            @pl.when(group < ACTIVE)
            def _():
                remote(
                    send_ref.at[pair], right_ref.at[:, me], a2a_send, a2a_recv,
                    (to_x, to_y, to_z, to_core),
                ).start()

    @pl.when(active)
    def _():
        pair = ACTIVE * (((z + 2) % 4) * 2 + core) + x * 8 + y * 2 + z_hi
        pltpu.make_async_copy(send_ref.at[pair], right_ref.at[:, me], own_sem.at[2]).start()

    send_right(1, 16)

    own_left.wait()
    wait_bytes(staged.at[0:7], l_recv.at[0])
    out_row, in_row = iotas(64, 64)
    sort_rows = ones_where(in_row == ((out_row & 7) << 3) + (out_row >> 3))
    wide = jnp.concatenate(
        [staged[:, g].astype(F32).reshape(64, LANE) for g in range(8)], axis=1
    ).astype(BF16)
    wide = dot(sort_rows, wide)
    for g in range(8):
        block = wide[:, LANE * g : LANE * g + LANE].reshape(8, 8, LANE).astype(BF16)
        bundle[8 * g : 8 * g + 8] = block
    own_bundle = pltpu.make_async_copy(
        bundle.at[0:LEFT_ROWS], left_ref.at[:, core, x, y], own_sem.at[0]
    )
    own_bundle.start()
    own_t.wait()
    wait_bytes(t_ref.at[0, 0, 0, 0], t_recv.at[0])

    @pl.loop(1, 4)
    def _(step):
        remote(
            bundle.at[0:half], left_ref.at[0:half, core, x, y], l_send.at[1], l_recv.at[1],
            (x, (y + step) % 4, z, core),
        ).start()
        remote(
            bundle.at[half:LEFT_ROWS], left_ref.at[half:LEFT_ROWS, core, x, y],
            l_send.at[2], l_recv.at[2], ((x + step) % 4, y, z, core),
        ).start()
        block = t_ref.at[core, y, :, x]
        to = ((x + step * core) % 4, (y + step * (1 - core)) % 4, z, core)
        remote(block, block, t_send.at[1], t_recv.at[1], to).start()

    send_right(16, 48)

    own_bundle.wait()
    three_bundles = left_ref.at[0:half, 0, 0, 0:3]
    three_rings = left_ref.at[0:half, 0, 0:3]
    wait_bytes(three_bundles, l_recv.at[1])
    wait_bytes(three_bundles, l_recv.at[2])
    wait_bytes(t_ref.at[0, 0, :, 0:3], t_recv.at[1])

    @pl.loop(1, 4)
    def _(step):
        block = left_ref.at[0:half, core, x]
        remote(block, block, l_send.at[3], l_recv.at[3], ((x + step) % 4, y, z, core)).start()
        block = left_ref.at[half:LEFT_ROWS, core, :, y]
        remote(block, block, l_send.at[4], l_recv.at[4], (x, (y + step) % 4, z, core)).start()

        @pl.when(core == 0)
        def _():
            block = t_ref.at[0, :, :, x]
            remote(block, block, t_send.at[2], t_recv.at[2], ((x + step) % 4, y, z, core)).start()

        @pl.when(core == 1)
        def _():
            block = t_ref.at[1, y]
            remote(block, block, t_send.at[2], t_recv.at[2], (x, (y + step) % 4, z, core)).start()

    send_right(48, 128)

    wait_bytes(three_rings, l_recv.at[3])
    wait_bytes(three_rings, l_recv.at[4])
    sibling = (x, y, z, 1 - core)
    block = left_ref.at[:, core]
    swap_left = remote(block, block, l_send.at[5], l_recv.at[5], sibling)
    swap_left.start()
    wait_bytes(t_ref.at[0, 0:3], t_recv.at[2])
    block = t_ref.at[core]
    swap_t = remote(block, block, t_send.at[3], t_recv.at[3], sibling)
    swap_t.start()

    send_right(128, 256)

    swap_left.wait()
    swap_t.wait()
    wait_bytes(staged.at[0:7], l_send.at[0])
    wait_bytes(three_bundles, l_send.at[1])
    wait_bytes(three_bundles, l_send.at[2])
    wait_bytes(three_rings, l_send.at[3])
    wait_bytes(three_rings, l_send.at[4])
    wait_bytes(t_ref.at[0, 0, 0, 0], t_send.at[0])
    wait_bytes(t_ref.at[0, 0, :, 0:3], t_send.at[1])
    wait_bytes(t_ref.at[0, 0:3], t_send.at[2])

    @pl.when(active)
    def _():
        wait_bytes(send_ref.at[0 : B_PAIRS - 1], a2a_send)
        wait_bytes(right_ref.at[:, 0], own_sem.at[2])
        wait_bytes(right_ref.at[:, 0 : DEVICES - 1], a2a_recv)

    @pl.when(jnp.logical_not(active))
    def _():
        wait_bytes(send_ref, a2a_send)


def compute_kernel(
    right_ref, left_ref, t_ref, out_ref, right_n, right_t, mid, blocks, send_sem, recv_sem
):
    x, y, z, core = place_of(lax.axis_index("row"), lax.axis_index("col"), lax.axis_index("depth"))
    group = x * 8 + y * 2 + z // 4
    barrier = pltpu.get_barrier_semaphore()

    def partner(step):
        return (x + step // 8) % 4, (y + step // 2) % 4, (z + 2 + 4 * (step % 2)) % 8

    @pl.loop(0, 32)
    def _(step):
        pl.semaphore_signal(
            barrier, inc=1, device_id=mesh_id(*partner(step), core),
            device_id_type=pl.DeviceIdType.MESH,
        )

    @pl.when(group < ACTIVE)
    def _():
        out_row, in_row = iotas(256, 256)
        sort_rows = ones_where(in_row == ((out_row & 31) << 3) + (out_row >> 5))
        row, column = iotas(LANE, LANE)
        identity = ones_where(row == column)
        for q in range(Q_LOCAL):
            for chunk in range(0, 8, 2):
                block = jnp.concatenate(
                    [
                        right_ref[q, 32 * c : 32 * c + 32].astype(F32).reshape(256, LANE)
                        for c in (chunk, chunk + 1)
                    ],
                    axis=1,
                )
                moved = dot(sort_rows, block.astype(BF16)).astype(BF16)
                for r in range(8):
                    for c in range(2):
                        base = 256 * q + 32 * (chunk + c)
                        right_n[r, base : base + 32, :] = moved[
                            32 * r : 32 * r + 32, LANE * c : LANE * c + LANE
                        ]
            for r in range(8):
                block = right_n[r, 256 * q : 256 * q + 256, :]
                right_t[LANE * r : LANE * r + LANE, 256 * q : 256 * q + 256] = dot_nt(
                    identity, block
                ).astype(BF16)
        for c in range(CW):
            left = jnp.concatenate(
                [
                    jnp.concatenate(
                        [
                            left_ref[12 * q + 4 * c + t].reshape(256, LANE)
                            for t in range(TILES)
                        ],
                        axis=1,
                    )
                    for q in range(Q_LOCAL)
                ],
                axis=0,
            )
            for m in range(4):
                which, half = divmod(m, 2)
                rebuilt = dot(right_t[256 * m : 256 * m + 256, :], left).astype(BF16)
                if c < 2:
                    for k in range(4):
                        base = (4 * half + k) * LANE + PAD * c
                        mid[which, base : base + PAD, :] = rebuilt[PAD * k : PAD * k + PAD]
                else:
                    base = 2 * NVP + 256 * half
                    mid[which, base : base + 256, :] = rebuilt

    pl.semaphore_wait(barrier, 32)

    @pl.when(group < ACTIVE)
    def _():
        first_half = lax.broadcasted_iota(jnp.int32, (ROWS_P, LANE), 1) < PAD

        @pl.loop(0, 4)
        def _(turn):
            to_x = (x + turn) % 4

            def tile(kind, k):
                return t_ref[kind, k // 2, k % 2, to_x].astype(F32).reshape(ROWS_P, LANE)

            tiles = [tile(0, k) for k in range(BLOCKS)]
            tiles += [tile(1, 2 * k) + tile(1, 2 * k + 1) for k in range(4)]
            t_rows = jnp.concatenate(tiles, axis=1).astype(BF16)
            totals = [dot(t_rows, mid[which]) for which in range(2)]
            for k in range(4):
                lanes = slice(LANE * k, LANE * k + LANE)
                one, two = totals[0][:, lanes], totals[1][:, lanes]
                even = jnp.where(first_half, one, pltpu.roll(two, PAD, 1))
                odd = jnp.where(first_half, pltpu.roll(one, PAD, 1), two)
                blocks[to_x, 2 * k] = even.reshape(GROUPS, 8, LANE).astype(BF16)
                blocks[to_x, 2 * k + 1] = odd.reshape(GROUPS, 8, LANE).astype(BF16)

            @pl.loop(0, 8)
            def _(step):
                _, to_y, to_z = partner(step)
                pltpu.make_async_remote_copy(
                    src_ref=blocks.at[to_x, to_y * 2 + to_z // 4],
                    dst_ref=out_ref.at[group],
                    send_sem=send_sem,
                    recv_sem=recv_sem,
                    device_id=mesh_id(to_x, to_y, to_z, core),
                    device_id_type=pl.DeviceIdType.MESH,
                ).start()

    wait_bytes(out_ref.at[0:ACTIVE], recv_sem)

    @pl.when(group < ACTIVE)
    def _():
        wait_bytes(blocks, send_sem)


def finish_kernel(in_ref, out_ref, turned):
    row, column = iotas(LANE, LANE)
    identity = ones_where(row == column)
    for group in range(ACTIVE):
        block = in_ref[group].astype(F32).reshape(ROWS_P, LANE).astype(BF16)
        turned[group] = dot_nt(identity, block)
    rows = 2 * ACTIVE * 8
    out_row, in_row = iotas(512, rows)
    sort_rows = ones_where(in_row == ((out_row & 63) << 3) + (out_row >> 6))
    for chunk in range(8):
        parts = []
        for group in range(ACTIVE):
            for which in range(2):
                base = PAD * which + 8 * chunk
                parts.append(turned[group, base : base + 8, :])
        moved = dot(sort_rows, jnp.concatenate(parts, axis=0).astype(BF16)).astype(BF16)
        for a in range(8 if chunk < 7 else 4):
            out_ref[8 * chunk + a] = moved[64 * a : 64 * a + 64][0:BLOCK, 0:ROWS_X]


def vmem(count):
    return [pl.BlockSpec(memory_space=pltpu.VMEM)] * count


def anywhere(count):
    return [pl.BlockSpec(memory_space=pl.ANY)] * count


def shape(*sizes):
    return jax.ShapeDtypeStruct(sizes, BF16)


def prepare(factors, amplitudes):
    t_local = jnp.pad(amplitudes.transpose(1, 0, 2), ((0, 0), (0, ROWS_P - ROWS_X), (0, 0)))
    return pl.pallas_call(
        prep_kernel,
        out_shape=(
            shape(B_PAIRS, Q_LOCAL, 8, LANE), shape(8, 8, LANE), shape(2, GROUPS, 8, LANE)
        ),
        in_specs=vmem(2),
        out_specs=tuple(vmem(3)),
        compiler_params=pltpu.CompilerParams(vmem_limit_bytes=40 * MIB),
        name="prepare",
    )(factors, t_local)


def exchange(send, left_own, t_own):
    dma = pltpu.SemaphoreType.DMA
    return pl.pallas_call(
        exchange_kernel,
        out_shape=(
            shape(Q_LOCAL, DEVICES, 8, LANE),
            shape(LEFT_ROWS, 2, 4, 4, 8, LANE),
            shape(2, 4, 2, 4, GROUPS, 8, LANE),
        ),
        in_specs=anywhere(3),
        out_specs=tuple(anywhere(3)),
        scratch_shapes=[
            pltpu.VMEM((8, 8, 8, LANE), BF16),
            pltpu.VMEM((64, 8, LANE), BF16),
            dma, dma, dma((6,)), dma((6,)), dma((4,)), dma((4,)), dma((3,)),
        ],
        compiler_params=pltpu.CompilerParams(has_side_effects=True, vmem_limit_bytes=4 * MIB),
        name="exchange",
    )(send, left_own, t_own)


def compute(right, left, t_full):
    dma = pltpu.SemaphoreType.DMA
    return pl.pallas_call(
        compute_kernel,
        out_shape=shape(32, GROUPS, 8, LANE),
        in_specs=vmem(3),
        out_specs=vmem(1)[0],
        scratch_shapes=[
            pltpu.VMEM((8, NAUX, LANE), BF16),
            pltpu.VMEM((2 * NVP, NAUX), BF16),
            pltpu.VMEM((2, KDIM, NVP), BF16),
            pltpu.VMEM((4, BLOCKS, GROUPS, 8, LANE), BF16),
            dma,
            dma,
        ],
        compiler_params=pltpu.CompilerParams(
            vmem_limit_bytes=28 * MIB, has_side_effects=True, collective_id=7
        ),
        name="compute",
    )(
        right,
        left.reshape(LEFT_ROWS, DEVICES // 8, 8, LANE),
        t_full,
    )


def finish(blocks):
    turned = pl.pallas_call(
        finish_kernel,
        out_shape=shape(BLOCK, BLOCK, ROWS_X),
        in_specs=vmem(1),
        out_specs=vmem(1)[0],
        scratch_shapes=[pltpu.VMEM((ACTIVE, LANE, ROWS_P), F32)],
        compiler_params=pltpu.CompilerParams(vmem_limit_bytes=40 * MIB),
        name="finish",
    )(blocks)
    return turned.transpose(2, 0, 1)


def on_device(factors, amplitudes):
    return finish(compute(*exchange(*prepare(factors, amplitudes))))


def solution(mesh):
    in_specs = (P(("row", "col", "depth"), None, None), P("row", None, "depth"))
    out_specs = P("row", "depth", "col")
    return jax.shard_map(
        on_device, mesh=mesh, in_specs=in_specs, out_specs=out_specs, check_vma=False
    )
```

time: 160 us -> 149 us (0.931); the launches traced: 160 us -> 147 us
  local copies, waits for them, and re-layouts: 10.1 us -> 2.78 us
  Pallas kernels: 150 us -> 144 us
    pallas_call x3 -> x2, Pallas kernels: 64 us -> 41.9 us  [the longest x1 38.8 us: compute(): pl.pallas_call(compute_kernel, out_shape=shape(32, GROUPS, 8, LANE), in_s...]
    pallas_call x1, Pallas kernels: 81.9 us -> 98.3 us  [exchange(): pl.pallas_call(exchange_kernel, out_shape=(shape(Q_LOCAL, DEVICES, 8, LAN...]
    unnamed x11 -> x3, local copies, waits for them, and re-layouts: 6.69 us -> 2.75 us
    pallas_call x1 -> x0, local copies, waits for them, and re-layouts: 3.38 us -> none  [finish(): pl.pallas_call(finish_kernel, out_shape=shape(ROWS_X, BLOCK, BLOCK), in_s...]
where the time goes in v2:
time: 149 us; the launch traced here: 147 us
  Pallas kernels  144 us (97%)
  local copies, waits for them, and re-layouts  2.78 us (2%)
    pallas_call x1, Pallas kernels, exchange(): pl.pallas_call(exchange_kernel, out_shape=(shape(Q_LOCAL, DEVICES, 8, LAN...  98.3 us
    pallas_call x1, Pallas kernels, compute(): pl.pallas_call(compute_kernel, out_shape=shape(32, GROUPS, 8, LANE), in_s...  38.8 us
    pallas_call x1, Pallas kernels, prepare(): pl.pallas_call(prep_kernel, out_shape=(shape(B_PAIRS, Q_LOCAL, 8, LANE),...  3.94 us
    pallas_call x1, Pallas kernels, finish(): pl.pallas_call(finish_kernel, out_shape=shape(BLOCK, BLOCK, ROWS_X), in_s...  3.12 us

profile of v2, /device:TPU:1, one launch (start us, length us, event | category | flops | bytes accessed | tf_op | source)
XLA Modules:
  0.0 147.0 jit_solution(4329032335682483369)
XLA Ops:
  0.0 1.1 copy.3
  1.1 0.0 copy-start
  1.1 1.7 %copy-done = bf16[5,480,480]{2,1,0:T(8,128)(2,1)S(1)} copy-done((bf16[5,480,480]{2,1,0:T(8,128)(2,1)S(1)}, bf16[5,480,480]{2,1,0:T(8,128)(2,1)}, u32[]{:S(2)}) %copy-start) | copy-done | bytes 2304024
  2.8 3.9 %prepare.1 = (bf16[240,5,8,128]{3,2,1,0:T(8,128)(2,1)S(1)}, bf16[8,8,128]{2,1,0:T(8,128)(2,1)S(1)}, bf16[2,17,8,128]{3,2,1,0:T(8,128)(2,1)S(1)}) custom-call(bf16[5,480,480]{2,1,0:T(8,128)(2,1)S(1)} %copy-done, bf16[3,136,60]{2,1,0:T(8,128)(2,1)S(1)} %pad.4.t_ref), custom_call_target="tpu_custom_call" | custom-call | tf_op jit(solution)/shard_map/prepare/pallas_call | solution.py:398
  6.7 98.3 %exchange.1 = (bf16[5,256,8,128]{3,2,1,0:T(8,128)(2,1)S(1)}, bf16[60,2,4,4,8,128]{5,4,3,2,1,0:T(8,128)(2,1)S(1)}, bf16[2,4,2,4,17,8,128]{6,5,4,3,2,1,0:T(8,128)(2,1)S(1)}) custom-call(bf16[240,5,8,128]{3,2,1,0:T(8,128)(2,1)S(1)} %get-tuple-element.11.send_ref, bf16[8,8,128]{2,1,0:T(8,128)(2,1)S(1)} %get-tuple-element.12.left_in, ...), custom_call_target="tpu_custom_call" | custom-call | tf_op jit(solution)/shard_map/exchange/pallas_call | solution.py:412
  105.1 38.8 %compute.1.in_ref = bf16[32,17,8,128]{3,2,1,0:T(8,128)(2,1)S(1)} custom-call(bf16[5,256,8,128]{3,2,1,0:T(8,128)(2,1)S(1)} %get-tuple-element.14.right_ref, bf16[60,32,8,128]{3,2,1,0:T(8,128)(2,1)S(1)} %bitcast.3, bf16[2,4,2,4,17,8,128]{6,5,4,3,2,1,0:T(8,128)(2,1)S(1)} %get-tuple-element.16.t_ref), custom_call_target="tpu_custom_call" | custom-call | tf_op jit(solution)/shard_map/compute/pallas_call | solution.py:433
  143.9 3.1 %finish.1 = bf16[60,60,132]{2,1,0:T(8,128)(2,1)} custom-call(bf16[32,17,8,128]{3,2,1,0:T(8,128)(2,1)S(1)} %compute.1.in_ref), custom_call_target="tpu_custom_call" | custom-call | tf_op jit(solution)/shard_map/finish/pallas_call | solution.py:458
  (1 shorter events, 0.0 us)
Async XLA Ops:
  1.1 1.7 %copy-start = (bf16[5,480,480]{2,1,0:T(8,128)(2,1)S(1)}, bf16[5,480,480]{2,1,0:T(8,128)(2,1)}, u32[]{:S(2)}) copy-start(bf16[5,480,480]{2,1,0:T(8,128)(2,1)} %f_ref.1) | copy-start | bytes 6912004

commit v3 on v2

--- a/solution.py
+++ b/solution.py
@@ -20,7 +20,10 @@
 GROUPS = 17
 ROWS_P = GROUPS * 8
 B_PAIRS = 240
-ACTIVE = 30
+SLOTS = 15
+ACTIVE = 2 * SLOTS
+ORDER = ((2, 1), (1, 1), (3, 1), (0, 1), (2, 0), (1, 0), (3, 0), "beside", "own")
+PARTS = len(ORDER)
 KDIM = CW * NVP
 LEFT_ROWS = Q_LOCAL * CW * TILES
 BF16 = jnp.bfloat16
@@ -51,7 +54,7 @@
     return ones_where((row == (column >> 6) * BLOCK + within) & (within < BLOCK))
 
 
-def prep_kernel(f_ref, t_ref, send_ref, left_ref, t_out_ref):
+def prepare(f_ref, t_ref, send_ref, left_ref, t_out_ref):
     spread = spread_matrix()
     out_row, in_row = iotas(LANE, LANE)
     gather_rows = ones_where(
@@ -91,6 +94,10 @@
     return row, depth // 2, (depth % 2) * 4 + col // 2, col % 2
 
 
+def slot_of(x, y):
+    return (y - x + 4) % 4 * 4 + x
+
+
 def mesh_id(x, y, z, core):
     return {"row": x, "col": (z % 4) * 2 + core, "depth": y * 2 + z // 4}
 
@@ -100,13 +107,27 @@
 
 
 def exchange_kernel(
-    send_ref, left_in, t_in, right_ref, left_ref, t_ref,
-    staged, bundle, a2a_send, a2a_recv, l_send, l_recv, t_send, t_recv, own_sem,
+    f_ref, t_local, right_ref, left_ref, t_ref,
+    send_ref, left_in, t_in, staged, bundle, relay, z_send, z_recv, xy_send, xy_recv,
+    l_send, l_recv, t_send, t_recv, own_sem, z_own, xy_own,
 ):
     x, y, z, core = place_of(lax.axis_index("row"), lax.axis_index("col"), lax.axis_index("depth"))
     z_hi = z // 4
-    me = core * 128 + x * 32 + y * 8 + z
-    active = x * 8 + y * 2 + z_hi < ACTIVE
+    active = slot_of(x, y) < SLOTS
+    barrier = pltpu.get_barrier_semaphore()
+
+    def greet(x, y, z, core):
+        pl.semaphore_signal(
+            barrier, inc=1, device_id=mesh_id(x, y, z, core), device_id_type=pl.DeviceIdType.MESH
+        )
+
+    @pl.loop(1, 16)
+    def _(step):
+        greet(x, y, (z + step) % 8, (core + step // 8) % 2)
+        greet((x + step // 4) % 4, (y + step) % 4, z, core)
+
+    prepare(f_ref, t_local, send_ref, left_in, t_in)
+    pl.semaphore_wait(barrier, 30)
     half = LEFT_ROWS // 2
 
     def remote(src, dst, send, recv, to):
@@ -129,29 +150,81 @@
             left_in, staged.at[z], l_send.at[0], l_recv.at[0], (x, y, (z + step) % 8, core)
         ).start()
 
-    def send_right(first, last):
-        @pl.loop(first, last)
-        def _(step):
-            to_z = (z + step) % 8
-            to_core = (core + step // 8) % 2
-            to_y = (y + step // 16) % 4
-            to_x = (x + step // 64) % 4
-            group = to_x * 8 + to_y * 2 + to_z // 4
-            pair = ACTIVE * (((to_z + 2) % 4) * 2 + to_core) + group
-
-            @pl.when(group < ACTIVE)
+    def width(part):
+        return 1 if isinstance(ORDER[part], str) else 2
+
+    def first_slot(part):
+        if ORDER[part] == "own":
+            return slot_of(x, y)
+        if ORDER[part] == "beside":
+            return slot_of(x, y) + 1 - 2 * (x % 2)
+        diagonal, other = ORDER[part]
+        return (y - x + diagonal + 4) % 4 * 4 + 2 * ((x // 2 + other) % 2)
+
+    def by_count(part, act):
+        short = first_slot(part) + width(part) > SLOTS
+        if width(part) > 1:
+
+            @pl.when(short)
+            def _():
+                act(width(part) - 1)
+
+        @pl.when(jnp.logical_not(short))
+        def _():
+            act(width(part))
+
+    def pair_at(to_z, to_core):
+        return ACTIVE * (((to_z + 2) % 4) * 2 + to_core) + SLOTS * (to_z // 4)
+
+    def send_along_z(part):
+        first = first_slot(part)
+
+        def send(count):
+            @pl.loop(1, 16)
+            def _(step):
+                to_z, to_core = (z + step) % 8, (core + step // 8) % 2
+                remote(
+                    send_ref.at[pl.ds(pair_at(to_z, to_core) + first, count)],
+                    relay.at[part, core, z, 0:count],
+                    z_send.at[part], z_recv.at[part], (x, y, to_z, to_core),
+                ).start()
+
+            pltpu.make_async_copy(
+                send_ref.at[pl.ds(pair_at(z, core) + first, count)],
+                relay.at[part, core, z, 0:count],
+                z_own.at[part],
+            ).start()
+
+        by_count(part, send)
+
+    def pass_on(part):
+        by_count(part, lambda count: wait_bytes(send_ref.at[0 : 15 * count], z_recv.at[part]))
+        by_count(part, lambda count: wait_bytes(send_ref.at[0:count], z_own.at[part]))
+
+        if ORDER[part] == "own":
+
+            @pl.when(active)
+            def _():
+                pltpu.make_async_copy(
+                    relay.at[part, :, :, 0], right_ref.at[:, x, y], xy_own
+                ).start()
+
+            return
+
+        @pl.loop(0, width(part))
+        def _(i):
+            slot = first_slot(part) + i
+            to_x = slot % 4
+
+            @pl.when(slot < SLOTS)
             def _():
                 remote(
-                    send_ref.at[pair], right_ref.at[:, me], a2a_send, a2a_recv,
-                    (to_x, to_y, to_z, to_core),
+                    relay.at[part, :, :, i], right_ref.at[:, x, y], xy_send.at[part],
+                    xy_recv.at[part], (to_x, (to_x + slot // 4) % 4, z, core),
                 ).start()
 
-    @pl.when(active)
-    def _():
-        pair = ACTIVE * (((z + 2) % 4) * 2 + core) + x * 8 + y * 2 + z_hi
-        pltpu.make_async_copy(send_ref.at[pair], right_ref.at[:, me], own_sem.at[2]).start()
-
-    send_right(1, 16)
+    send_along_z(0)
+    send_along_z(1)
 
     own_left.wait()
     wait_bytes(staged.at[0:7], l_recv.at[0])
@@ -185,7 +258,9 @@
         to = ((x + step * core) % 4, (y + step * (1 - core)) % 4, z, core)
         remote(block, block, t_send.at[1], t_recv.at[1], to).start()
 
-    send_right(16, 48)
+    send_along_z(2)
+    pass_on(0)
+    send_along_z(3)
 
     own_bundle.wait()
     three_bundles = left_ref.at[0:half, 0, 0, 0:3]
@@ -211,7 +286,14 @@
             block = t_ref.at[1, y]
             remote(block, block, t_send.at[2], t_recv.at[2], (x, (y + step) % 4, z, core)).start()
 
-    send_right(48, 128)
+    send_along_z(4)
+    pass_on(1)
+    send_along_z(5)
+    pass_on(2)
+    send_along_z(6)
+    pass_on(3)
+    send_along_z(7)
+    send_along_z(8)
 
     wait_bytes(three_rings, l_recv.at[3])
     wait_bytes(three_rings, l_recv.at[4])
@@ -224,7 +306,8 @@
     swap_t = remote(block, block, t_send.at[3], t_recv.at[3], sibling)
     swap_t.start()
 
-    send_right(128, 256)
+    for part in range(4, PARTS):
+        pass_on(part)
 
     swap_left.wait()
     swap_t.wait()
@@ -237,22 +320,28 @@
     wait_bytes(t_ref.at[0, 0, :, 0:3], t_send.at[1])
     wait_bytes(t_ref.at[0, 0:3], t_send.at[2])
 
+    for part in range(PARTS):
+        by_count(part, lambda count: wait_bytes(send_ref.at[0 : 15 * count], z_send.at[part]))
+
+    def columns(count):
+        return right_ref.at[:, 0, 0:count]
+
+    for part in range(PARTS - 1):
+        by_count(part, lambda count: wait_bytes(columns(count), xy_send.at[part]))
+
     @pl.when(active)
     def _():
-        wait_bytes(send_ref.at[0 : B_PAIRS - 1], a2a_send)
-        wait_bytes(right_ref.at[:, 0], own_sem.at[2])
-        wait_bytes(right_ref.at[:, 0 : DEVICES - 1], a2a_recv)
-
-    @pl.when(jnp.logical_not(active))
-    def _():
-        wait_bytes(send_ref, a2a_send)
+        wait_bytes(columns(1), xy_own)
+        for part in range(PARTS - 1):
+            wait_bytes(columns(width(part)), xy_recv.at[part])
 
 
 def compute_kernel(
     right_ref, left_ref, t_ref, out_ref, right_n, right_t, mid, blocks, send_sem, recv_sem
 ):
     x, y, z, core = place_of(lax.axis_index("row"), lax.axis_index("col"), lax.axis_index("depth"))
-    group = x * 8 + y * 2 + z // 4
+    group = SLOTS * (z // 4) + slot_of(x, y)
+    active = slot_of(x, y) < SLOTS
     barrier = pltpu.get_barrier_semaphore()
 
     def partner(step):
@@ -265,7 +354,7 @@
             device_id_type=pl.DeviceIdType.MESH,
         )
 
-    @pl.when(group < ACTIVE)
+    @pl.when(active)
     def _():
         out_row, in_row = iotas(256, 256)
         sort_rows = ones_where(in_row == ((out_row & 31) << 3) + (out_row >> 5))
@@ -275,7 +364,7 @@
             for chunk in range(0, 8, 2):
                 block = jnp.concatenate(
                     [
-                        right_ref[q, 32 * c : 32 * c + 32].astype(F32).reshape(256, LANE)
+                        right_ref[32 * c : 32 * c + 32, q].astype(F32).reshape(256, LANE)
                         for c in (chunk, chunk + 1)
                     ],
                     axis=1,
@@ -319,7 +408,7 @@
 
     pl.semaphore_wait(barrier, 32)
 
-    @pl.when(group < ACTIVE)
+    @pl.when(active)
     def _():
         first_half = lax.broadcasted_iota(jnp.int32, (ROWS_P, LANE), 1) < PAD
 
@@ -356,7 +445,7 @@
 
     wait_bytes(out_ref.at[0:ACTIVE], recv_sem)
 
-    @pl.when(group < ACTIVE)
+    @pl.when(active)
     def _():
         wait_bytes(blocks, send_sem)
 
@@ -393,39 +482,33 @@
     return jax.ShapeDtypeStruct(sizes, BF16)
 
 
-def prepare(factors, amplitudes):
+def exchange(factors, amplitudes):
+    dma = pltpu.SemaphoreType.DMA
     t_local = jnp.pad(amplitudes.transpose(1, 0, 2), ((0, 0), (0, ROWS_P - ROWS_X), (0, 0)))
-    return pl.pallas_call(
-        prep_kernel,
-        out_shape=(
-            shape(B_PAIRS, Q_LOCAL, 8, LANE), shape(8, 8, LANE), shape(2, GROUPS, 8, LANE)
-        ),
-        in_specs=vmem(2),
-        out_specs=tuple(vmem(3)),
-        compiler_params=pltpu.CompilerParams(vmem_limit_bytes=40 * MIB),
-        name="prepare",
-    )(factors, t_local)
-
-
-def exchange(send, left_own, t_own):
-    dma = pltpu.SemaphoreType.DMA
     return pl.pallas_call(
         exchange_kernel,
         out_shape=(
-            shape(Q_LOCAL, DEVICES, 8, LANE),
+            shape(2, 4, 4, 8, Q_LOCAL, 8, LANE),
             shape(LEFT_ROWS, 2, 4, 4, 8, LANE),
             shape(2, 4, 2, 4, GROUPS, 8, LANE),
         ),
-        in_specs=anywhere(3),
+        in_specs=vmem(2),
         out_specs=tuple(anywhere(3)),
         scratch_shapes=[
+            pltpu.VMEM((B_PAIRS, Q_LOCAL, 8, LANE), BF16),
+            pltpu.VMEM((8, 8, LANE), BF16),
+            pltpu.VMEM((2, GROUPS, 8, LANE), BF16),
             pltpu.VMEM((8, 8, 8, LANE), BF16),
             pltpu.VMEM((64, 8, LANE), BF16),
-            dma, dma, dma((6,)), dma((6,)), dma((4,)), dma((4,)), dma((3,)),
+            pltpu.VMEM((PARTS, 2, 8, 2, Q_LOCAL, 8, LANE), BF16),
+            dma((PARTS,)), dma((PARTS,)), dma((PARTS,)), dma((PARTS,)),
+            dma((6,)), dma((6,)), dma((4,)), dma((4,)), dma((2,)), dma((PARTS,)), dma,
         ],
-        compiler_params=pltpu.CompilerParams(has_side_effects=True, vmem_limit_bytes=4 * MIB),
+        compiler_params=pltpu.CompilerParams(
+            has_side_effects=True, vmem_limit_bytes=16 * MIB, collective_id=5
+        ),
         name="exchange",
-    )(send, left_own, t_own)
+    )(factors, t_local)
 
 
 def compute(right, left, t_full):
@@ -448,7 +531,7 @@
         ),
         name="compute",
     )(
-        right,
+        right.reshape(DEVICES, Q_LOCAL, 8, LANE),
         left.reshape(LEFT_ROWS, DEVICES // 8, 8, LANE),
         t_full,
     )
@@ -468,7 +551,7 @@
 
 
 def on_device(factors, amplitudes):
-    return finish(compute(*exchange(*prepare(factors, amplitudes))))
+    return finish(compute(*exchange(factors, amplitudes)))
 
 
 def solution(mesh):

time: 149 us -> 127 us (0.85); the launches traced: 147 us -> 127 us
  Pallas kernels: 144 us -> 124 us
    pallas_call x2 -> x1, Pallas kernels: 102 us -> 82.7 us  [exchange(): pl.pallas_call(exchange_kernel, out_shape=(shape(2, 4, 4, 8, Q_LOCAL, 8,...]
where the time goes in v3:
time: 127 us
  Pallas kernels  124 us (98%)
  local copies, waits for them, and re-layouts  2.78 us (2%)
    pallas_call x1, Pallas kernels, exchange(): pl.pallas_call(exchange_kernel, out_shape=(shape(2, 4, 4, 8, Q_LOCAL, 8,...  82.7 us
    pallas_call x1, Pallas kernels, compute(): pl.pallas_call(compute_kernel, out_shape=shape(32, GROUPS, 8, LANE), in_s...  38.6 us
    pallas_call x1, Pallas kernels, finish(): pl.pallas_call(finish_kernel, out_shape=shape(BLOCK, BLOCK, ROWS_X), in_s...  3.12 us
    unnamed x3, local copies, waits for them, and re-layouts  2.75 us

profile of v3, /device:TPU:1, one launch (start us, length us, event | category | flops | bytes accessed | tf_op | source)
XLA Modules:
  0.0 127.3 jit_solution(10313186005085496907)
XLA Ops:
  0.0 1.1 copy.3
  1.1 0.0 copy-start
  1.1 1.7 %copy-done = bf16[5,480,480]{2,1,0:T(8,128)(2,1)S(1)} copy-done((bf16[5,480,480]{2,1,0:T(8,128)(2,1)S(1)}, bf16[5,480,480]{2,1,0:T(8,128)(2,1)}, u32[]{:S(2)}) %copy-start) | copy-done | bytes 2304024
  2.8 82.7 %exchange.1 = (bf16[2,4,4,8,5,8,128]{6,5,4,3,2,1,0:T(8,128)(2,1)S(1)}, bf16[60,2,4,4,8,128]{5,4,3,2,1,0:T(8,128)(2,1)S(1)}, bf16[2,4,2,4,17,8,128]{6,5,4,3,2,1,0:T(8,128)(2,1)S(1)}) custom-call(bf16[5,480,480]{2,1,0:T(8,128)(2,1)S(1)} %copy-done, bf16[3,136,60]{2,1,0:T(8,128)(2,1)S(1)} %pad.4.t_local), custom_call_target="tpu_custom_call" | custom-call | tf_op jit(solution)/shard_map/exchange/pallas_call | solution.py:488
  85.5 38.6 %compute.1.in_ref = bf16[32,17,8,128]{3,2,1,0:T(8,128)(2,1)S(1)} custom-call(bf16[256,5,8,128]{3,2,1,0:T(8,128)(2,1)S(1)} %bitcast.5, bf16[60,32,8,128]{3,2,1,0:T(8,128)(2,1)S(1)} %bitcast.4, bf16[2,4,2,4,17,8,128]{6,5,4,3,2,1,0:T(8,128)(2,1)S(1)} %get-tuple-element.10.t_ref), custom_call_target="tpu_custom_call" | custom-call | tf_op jit(solution)/shard_map/compute/pallas_call | solution.py:516
  124.1 3.1 %finish.1 = bf16[60,60,132]{2,1,0:T(8,128)(2,1)} custom-call(bf16[32,17,8,128]{3,2,1,0:T(8,128)(2,1)S(1)} %compute.1.in_ref), custom_call_target="tpu_custom_call" | custom-call | tf_op jit(solution)/shard_map/finish/pallas_call | solution.py:541
  (1 shorter events, 0.0 us)
Async XLA Ops:
  1.1 1.7 %copy-start = (bf16[5,480,480]{2,1,0:T(8,128)(2,1)S(1)}, bf16[5,480,480]{2,1,0:T(8,128)(2,1)}, u32[]{:S(2)}) copy-start(bf16[5,480,480]{2,1,0:T(8,128)(2,1)} %f_ref.1) | copy-start | bytes 6912004

commit v4 on v3

--- a/solution.py
+++ b/solution.py
@@ -19,11 +19,14 @@
 ROWS_X = 132
 GROUPS = 17
 ROWS_P = GROUPS * 8
+FOLD = 72
+T_TILES = (GROUPS + FOLD // 8) // 2
 B_PAIRS = 240
 SLOTS = 15
 ACTIVE = 2 * SLOTS
-ORDER = ((2, 1), (1, 1), (3, 1), (0, 1), (2, 0), (1, 0), (3, 0), "beside", "own")
+ORDER = ((2, 0), (2, 1), (1, 0), (1, 1), (3, 0), (3, 1), (0, 1), "beside", "own")
 PARTS = len(ORDER)
+GROUPED = (range(0, 5), range(5, 7), range(7, 9))
 KDIM = CW * NVP
 LEFT_ROWS = Q_LOCAL * CW * TILES
 BF16 = jnp.bfloat16
@@ -80,14 +83,14 @@
         & ((in_row & 15) < CW)
     )
     left_ref[...] = dot(place, jnp.concatenate(left_tiles, axis=0)).reshape(8, 8, LANE).astype(BF16)
-    z_hi = lax.rem(lax.axis_index("depth"), 2)
     row, column = iotas(BLOCK, LANE)
     low = ones_where(row == column)
     high = ones_where(row + PAD == column)
-    either = ones_where(row + PAD * z_hi == column)
-    both = dot(t_ref[0], low) + dot(t_ref[1], high)
-    t_out_ref[0] = both.reshape(GROUPS, 8, LANE).astype(BF16)
-    t_out_ref[1] = dot(t_ref[2], either).reshape(GROUPS, 8, LANE).astype(BF16)
+    both = (dot(t_ref[0], low) + dot(t_ref[1], high)).reshape(GROUPS, 8, LANE).astype(BF16)
+    folded = dot(t_ref[2], low)[0:FOLD] + dot(t_ref[2], high)[ROWS_P - FOLD : ROWS_P]
+    t_out_ref[0] = both[0:T_TILES]
+    t_out_ref[1, 0 : GROUPS - T_TILES] = both[T_TILES:GROUPS]
+    t_out_ref[1, GROUPS - T_TILES : T_TILES] = folded.reshape(FOLD // 8, 8, LANE).astype(BF16)
 
 
 def place_of(row, col, depth):
@@ -106,10 +109,12 @@
     pltpu.make_async_copy(ref, ref, sem).wait()
 
 
-def exchange_kernel(
-    f_ref, t_local, right_ref, left_ref, t_ref,
-    send_ref, left_in, t_in, staged, bundle, relay, z_send, z_recv, xy_send, xy_recv,
-    l_send, l_recv, t_send, t_recv, own_sem, z_own, xy_own,
+def ladder_kernel(
+    f_ref, t_local, out_ref,
+    send_ref, left_in, t_in, staged, bundle, relay, right_ref, left_ref, t_ref,
+    left_rows, right_n, right_t, total, mid, blocks,
+    z_send, z_recv, xy_send, xy_recv, l_send, l_recv, t_send, t_recv, own_sem, z_own, xy_own,
+    out_send, out_recv,
 ):
     x, y, z, core = place_of(lax.axis_index("row"), lax.axis_index("col"), lax.axis_index("depth"))
     z_hi = z // 4
@@ -125,9 +130,11 @@
     def _(step):
         greet(x, y, (z + step) % 8, (core + step // 8) % 2)
         greet((x + step // 4) % 4, (y + step) % 4, z, core)
+        greet((x + step // 4) % 4, (y + step) % 4, (z + 2) % 8, core)
+        greet((x + step // 4) % 4, (y + step) % 4, (z + 6) % 8, core)
 
     prepare(f_ref, t_local, send_ref, left_in, t_in)
-    pl.semaphore_wait(barrier, 30)
+    pl.semaphore_wait(barrier, 60)
     half = LEFT_ROWS // 2
 
     def remote(src, dst, send, recv, to):
@@ -206,7 +213,7 @@
             @pl.when(active)
             def _():
                 pltpu.make_async_copy(
-                    relay.at[part, :, :, 0], right_ref.at[:, x, y], xy_own
+                    relay.at[part, :, :, 0], right_ref.at[x, y], xy_own
                 ).start()
 
             return
@@ -219,7 +226,7 @@
             @pl.when(slot < SLOTS)
             def _():
                 remote(
-                    relay.at[part, :, :, i], right_ref.at[:, x, y], xy_send.at[part],
+                    relay.at[part, :, :, i], right_ref.at[x, y], xy_send.at[part],
                     xy_recv.at[part], (to_x, (to_x + slot // 4) % 4, z, core),
                 ).start()
 
@@ -238,7 +245,7 @@
         block = wide[:, LANE * g : LANE * g + LANE].reshape(8, 8, LANE).astype(BF16)
         bundle[8 * g : 8 * g + 8] = block
     own_bundle = pltpu.make_async_copy(
-        bundle.at[0:LEFT_ROWS], left_ref.at[:, core, x, y], own_sem.at[0]
+        bundle.at[0:LEFT_ROWS], left_ref.at[:, x, y, core], own_sem.at[0]
     )
     own_bundle.start()
     own_t.wait()
@@ -247,11 +254,11 @@
     @pl.loop(1, 4)
     def _(step):
         remote(
-            bundle.at[0:half], left_ref.at[0:half, core, x, y], l_send.at[1], l_recv.at[1],
+            bundle.at[0:half], left_ref.at[0:half, x, y, core], l_send.at[1], l_recv.at[1],
             (x, (y + step) % 4, z, core),
         ).start()
         remote(
-            bundle.at[half:LEFT_ROWS], left_ref.at[half:LEFT_ROWS, core, x, y],
+            bundle.at[half:LEFT_ROWS], left_ref.at[half:LEFT_ROWS, x, y, core],
             l_send.at[2], l_recv.at[2], ((x + step) % 4, y, z, core),
         ).start()
         block = t_ref.at[core, y, :, x]
@@ -263,17 +270,17 @@
     send_along_z(3)
 
     own_bundle.wait()
-    three_bundles = left_ref.at[0:half, 0, 0, 0:3]
-    three_rings = left_ref.at[0:half, 0, 0:3]
+    three_bundles = left_ref.at[0:half, 0, 0:3, 0]
+    three_rings = left_ref.at[0:half, 0:3, :, 0]
     wait_bytes(three_bundles, l_recv.at[1])
     wait_bytes(three_bundles, l_recv.at[2])
     wait_bytes(t_ref.at[0, 0, :, 0:3], t_recv.at[1])
 
     @pl.loop(1, 4)
     def _(step):
-        block = left_ref.at[0:half, core, x]
+        block = left_ref.at[0:half, x, :, core]
         remote(block, block, l_send.at[3], l_recv.at[3], ((x + step) % 4, y, z, core)).start()
-        block = left_ref.at[half:LEFT_ROWS, core, :, y]
+        block = left_ref.at[half:LEFT_ROWS, :, y, core]
         remote(block, block, l_send.at[4], l_recv.at[4], (x, (y + step) % 4, z, core)).start()
 
         @pl.when(core == 0)
@@ -298,7 +305,7 @@
     wait_bytes(three_rings, l_recv.at[3])
     wait_bytes(three_rings, l_recv.at[4])
     sibling = (x, y, z, 1 - core)
-    block = left_ref.at[:, core]
+    block = left_ref.at[:, :, :, core]
     swap_left = remote(block, block, l_send.at[5], l_recv.at[5], sibling)
     swap_left.start()
     wait_bytes(t_ref.at[0, 0:3], t_recv.at[2])
@@ -306,121 +313,144 @@
     swap_t = remote(block, block, t_send.at[3], t_recv.at[3], sibling)
     swap_t.start()
 
-    for part in range(4, PARTS):
-        pass_on(part)
-
-    swap_left.wait()
-    swap_t.wait()
-    wait_bytes(staged.at[0:7], l_send.at[0])
-    wait_bytes(three_bundles, l_send.at[1])
-    wait_bytes(three_bundles, l_send.at[2])
-    wait_bytes(three_rings, l_send.at[3])
-    wait_bytes(three_rings, l_send.at[4])
-    wait_bytes(t_ref.at[0, 0, 0, 0], t_send.at[0])
-    wait_bytes(t_ref.at[0, 0, :, 0:3], t_send.at[1])
-    wait_bytes(t_ref.at[0, 0:3], t_send.at[2])
-
-    for part in range(PARTS):
-        by_count(part, lambda count: wait_bytes(send_ref.at[0 : 15 * count], z_send.at[part]))
-
     def columns(count):
-        return right_ref.at[:, 0, 0:count]
-
-    for part in range(PARTS - 1):
-        by_count(part, lambda count: wait_bytes(columns(count), xy_send.at[part]))
-
-    @pl.when(active)
-    def _():
-        wait_bytes(columns(1), xy_own)
-        for part in range(PARTS - 1):
-            wait_bytes(columns(width(part)), xy_recv.at[part])
-
-
-def compute_kernel(
-    right_ref, left_ref, t_ref, out_ref, right_n, right_t, mid, blocks, send_sem, recv_sem
-):
-    x, y, z, core = place_of(lax.axis_index("row"), lax.axis_index("col"), lax.axis_index("depth"))
-    group = SLOTS * (z // 4) + slot_of(x, y)
-    active = slot_of(x, y) < SLOTS
-    barrier = pltpu.get_barrier_semaphore()
-
-    def partner(step):
-        return (x + step // 8) % 4, (y + step // 2) % 4, (z + 2 + 4 * (step % 2)) % 8
-
-    @pl.loop(0, 32)
-    def _(step):
-        pl.semaphore_signal(
-            barrier, inc=1, device_id=mesh_id(*partner(step), core),
-            device_id_type=pl.DeviceIdType.MESH,
-        )
-
-    @pl.when(active)
-    def _():
-        out_row, in_row = iotas(256, 256)
-        sort_rows = ones_where(in_row == ((out_row & 31) << 3) + (out_row >> 5))
-        row, column = iotas(LANE, LANE)
-        identity = ones_where(row == column)
-        for q in range(Q_LOCAL):
-            for chunk in range(0, 8, 2):
+        return right_ref.at[0, 0:count]
+
+    out_row, in_row = iotas(256, 256)
+    sort_rows = ones_where(in_row == ((out_row & 31) << 3) + (out_row >> 5))
+    row, column = iotas(LANE, LANE)
+    identity = ones_where(row == column)
+
+    def sources(part):
+        diagonal, other = (0, 0) if isinstance(ORDER[part], str) else ORDER[part]
+        diagonal = (y - x - diagonal + 8) % 4
+        from_x = 2 * ((x // 2 + other) % 2)
+        return [(from_x + i, (from_x + i + diagonal) % 4) for i in range(2)]
+
+    def pairs_of(group):
+        return [part for part in GROUPED[group] if ORDER[part] != "own"]
+
+    def sort_group(group):
+        pairs = pairs_of(group)
+        for chunk, part in enumerate(pairs):
+            froms = sources(part)
+            for q in range(Q_LOCAL):
+                base = 32 * (Q_LOCAL * chunk + q)
                 block = jnp.concatenate(
                     [
-                        right_ref[32 * c : 32 * c + 32, q].astype(F32).reshape(256, LANE)
-                        for c in (chunk, chunk + 1)
+                        right_ref[from_x, from_y, :, :, q].astype(F32).reshape(LANE, LANE)
+                        for from_x, from_y in froms
                     ],
-                    axis=1,
+                    axis=0,
                 )
                 moved = dot(sort_rows, block.astype(BF16)).astype(BF16)
                 for r in range(8):
-                    for c in range(2):
-                        base = 256 * q + 32 * (chunk + c)
-                        right_n[r, base : base + 32, :] = moved[
-                            32 * r : 32 * r + 32, LANE * c : LANE * c + LANE
-                        ]
-            for r in range(8):
-                block = right_n[r, 256 * q : 256 * q + 256, :]
-                right_t[LANE * r : LANE * r + LANE, 256 * q : 256 * q + 256] = dot_nt(
-                    identity, block
-                ).astype(BF16)
-        for c in range(CW):
-            left = jnp.concatenate(
-                [
-                    jnp.concatenate(
-                        [
-                            left_ref[12 * q + 4 * c + t].reshape(256, LANE)
-                            for t in range(TILES)
-                        ],
-                        axis=1,
-                    )
-                    for q in range(Q_LOCAL)
-                ],
-                axis=0,
-            )
-            for m in range(4):
-                which, half = divmod(m, 2)
-                rebuilt = dot(right_t[256 * m : 256 * m + 256, :], left).astype(BF16)
+                    right_n[r, base : base + 32, :] = moved[32 * r : 32 * r + 32]
+        depth = 32 * Q_LOCAL * len(pairs)
+        for r in range(8):
+            right_t[LANE * r : LANE * r + LANE, 0:depth] = dot_nt(
+                identity, right_n[r, 0:depth, :]
+            ).astype(BF16)
+
+    def gather_left(group):
+        for chunk, part in enumerate(pairs_of(group)):
+            for i, (from_x, from_y) in enumerate(sources(part)):
+                for r in range(LEFT_ROWS):
+                    q, tile = divmod(r, CW * TILES)
+                    base = 32 * (Q_LOCAL * chunk + q) + 16 * i
+                    left_rows[base : base + 16, LANE * tile : LANE * tile + LANE] = left_ref[
+                        r, from_x, from_y
+                    ].reshape(16, LANE)
+
+    def multiply(group):
+        depth = 32 * Q_LOCAL * len(pairs_of(group))
+        for m in range(4):
+            which, half_of_d = divmod(m, 2)
+            for c in range(CW):
+                rows, lanes = slice(256 * m, 256 * m + 256), slice(NVP * c, NVP * c + NVP)
+                rebuilt = dot(right_t[rows, 0:depth], left_rows[0:depth, lanes])
+                if group > 0:
+                    rebuilt += total[rows, lanes]
+                if group < len(GROUPED) - 1:
+                    total[rows, lanes] = rebuilt
+                    continue
+                rebuilt = rebuilt.astype(BF16)
                 if c < 2:
                     for k in range(4):
-                        base = (4 * half + k) * LANE + PAD * c
+                        base = (4 * half_of_d + k) * LANE + PAD * c
                         mid[which, base : base + PAD, :] = rebuilt[PAD * k : PAD * k + PAD]
                 else:
-                    base = 2 * NVP + 256 * half
+                    base = 2 * NVP + 256 * half_of_d
                     mid[which, base : base + 256, :] = rebuilt
 
-    pl.semaphore_wait(barrier, 32)
+    def arrived(parts):
+        for part in parts:
+            if ORDER[part] == "own":
+                wait_bytes(columns(1), xy_own)
+            else:
+                wait_bytes(columns(width(part)), xy_recv.at[part])
+
+    pass_on(4)
+    pass_on(5)
 
     @pl.when(active)
     def _():
+        arrived(GROUPED[0])
+        sort_group(0)
+
+    pass_on(6)
+    swap_left.wait_recv()
+
+    @pl.when(active)
+    def _():
+        gather_left(0)
+        multiply(0)
+
+    pass_on(7)
+
+    @pl.when(active)
+    def _():
+        arrived(GROUPED[1])
+        sort_group(1)
+        gather_left(1)
+        multiply(1)
+
+    pass_on(8)
+    swap_t.wait_recv()
+    slot = SLOTS * z_hi + slot_of(x, y)
+
+    @pl.when(active)
+    def _():
+        gather_left(2)
+        arrived(GROUPED[2])
+        sort_group(2)
+        multiply(2)
         first_half = lax.broadcasted_iota(jnp.int32, (ROWS_P, LANE), 1) < PAD
 
         @pl.loop(0, 4)
         def _(turn):
             to_x = (x + turn) % 4
 
-            def tile(kind, k):
-                return t_ref[kind, k // 2, k % 2, to_x].astype(F32).reshape(ROWS_P, LANE)
-
-            tiles = [tile(0, k) for k in range(BLOCKS)]
-            tiles += [tile(1, 2 * k) + tile(1, 2 * k + 1) for k in range(4)]
+            def tiles_of(half, k, first, last):
+                return t_ref[half, k // 2, k % 2, to_x, first:last].astype(F32)
+
+            def side_by_side(k):
+                rest = GROUPS - T_TILES
+                whole = [tiles_of(0, k, 0, T_TILES), tiles_of(1, k, 0, rest)]
+                return jnp.concatenate(whole, axis=0).reshape(ROWS_P, LANE)
+
+            def unfolded(k):
+                one, two = (
+                    tiles_of(1, k + i, GROUPS - T_TILES, T_TILES).reshape(FOLD, LANE)
+                    for i in range(2)
+                )
+                begin = first_half[0:FOLD]
+                top = jnp.where(begin, one, pltpu.roll(two, PAD, 1))
+                bottom = jnp.where(begin, pltpu.roll(one, PAD, 1), two)
+                return jnp.concatenate([top, bottom[2 * FOLD - ROWS_P : FOLD]], axis=0)
+
+            tiles = [side_by_side(k) for k in range(BLOCKS)]
+            tiles += [unfolded(2 * k) for k in range(4)]
             t_rows = jnp.concatenate(tiles, axis=1).astype(BF16)
             totals = [dot(t_rows, mid[which]) for which in range(2)]
             for k in range(4):
@@ -433,22 +463,38 @@
 
             @pl.loop(0, 8)
             def _(step):
-                _, to_y, to_z = partner(step)
+                to_y, to_z = (y + step // 2) % 4, (z + 2 + 4 * (step % 2)) % 8
                 pltpu.make_async_remote_copy(
                     src_ref=blocks.at[to_x, to_y * 2 + to_z // 4],
-                    dst_ref=out_ref.at[group],
-                    send_sem=send_sem,
-                    recv_sem=recv_sem,
+                    dst_ref=out_ref.at[slot],
+                    send_sem=out_send,
+                    recv_sem=out_recv,
                     device_id=mesh_id(to_x, to_y, to_z, core),
                     device_id_type=pl.DeviceIdType.MESH,
                 ).start()
 
-    wait_bytes(out_ref.at[0:ACTIVE], recv_sem)
+    wait_bytes(out_ref.at[0:ACTIVE], out_recv)
 
     @pl.when(active)
     def _():
-        wait_bytes(blocks, send_sem)
-
+        wait_bytes(blocks, out_send)
+
+    swap_left.wait_send()
+    swap_t.wait_send()
+    wait_bytes(staged.at[0:7], l_send.at[0])
+    wait_bytes(three_bundles, l_send.at[1])
+    wait_bytes(three_bundles, l_send.at[2])
+    wait_bytes(three_rings, l_send.at[3])
+    wait_bytes(three_rings, l_send.at[4])
+    wait_bytes(t_ref.at[0, 0, 0, 0], t_send.at[0])
+    wait_bytes(t_ref.at[0, 0, :, 0:3], t_send.at[1])
+    wait_bytes(t_ref.at[0, 0:3], t_send.at[2])
+
+    for part in range(PARTS):
+        by_count(part, lambda count: wait_bytes(send_ref.at[0 : 15 * count], z_send.at[part]))
+
+    for part in range(PARTS - 1):
+        by_count(part, lambda count: wait_bytes(columns(count), xy_send.at[part]))
 
 def finish_kernel(in_ref, out_ref, turned):
     row, column = iotas(LANE, LANE)
@@ -482,59 +528,40 @@
     return jax.ShapeDtypeStruct(sizes, BF16)
 
 
-def exchange(factors, amplitudes):
+def ladder(factors, amplitudes):
     dma = pltpu.SemaphoreType.DMA
     t_local = jnp.pad(amplitudes.transpose(1, 0, 2), ((0, 0), (0, ROWS_P - ROWS_X), (0, 0)))
+    deepest = 32 * Q_LOCAL * 5
     return pl.pallas_call(
-        exchange_kernel,
-        out_shape=(
-            shape(2, 4, 4, 8, Q_LOCAL, 8, LANE),
-            shape(LEFT_ROWS, 2, 4, 4, 8, LANE),
-            shape(2, 4, 2, 4, GROUPS, 8, LANE),
-        ),
+        ladder_kernel,
+        out_shape=shape(32, GROUPS, 8, LANE),
         in_specs=vmem(2),
-        out_specs=tuple(anywhere(3)),
+        out_specs=vmem(1)[0],
         scratch_shapes=[
             pltpu.VMEM((B_PAIRS, Q_LOCAL, 8, LANE), BF16),
             pltpu.VMEM((8, 8, LANE), BF16),
-            pltpu.VMEM((2, GROUPS, 8, LANE), BF16),
+            pltpu.VMEM((2, T_TILES, 8, LANE), BF16),
             pltpu.VMEM((8, 8, 8, LANE), BF16),
             pltpu.VMEM((64, 8, LANE), BF16),
             pltpu.VMEM((PARTS, 2, 8, 2, Q_LOCAL, 8, LANE), BF16),
+            pltpu.VMEM((4, 4, 2, 8, Q_LOCAL, 8, LANE), BF16),
+            pltpu.VMEM((LEFT_ROWS, 4, 4, 2, 8, LANE), BF16),
+            pltpu.VMEM((2, 4, 2, 4, T_TILES, 8, LANE), BF16),
+            pltpu.VMEM((deepest, KDIM), BF16),
+            pltpu.VMEM((8, deepest, LANE), BF16),
+            pltpu.VMEM((2 * NVP, deepest + 96), BF16),
+            pltpu.VMEM((2 * NVP, KDIM), F32),
+            pltpu.VMEM((2, KDIM, NVP), BF16),
+            pltpu.VMEM((4, BLOCKS, GROUPS, 8, LANE), BF16),
             dma((PARTS,)), dma((PARTS,)), dma((PARTS,)), dma((PARTS,)),
             dma((6,)), dma((6,)), dma((4,)), dma((4,)), dma((2,)), dma((PARTS,)), dma,
+            dma, dma,
         ],
         compiler_params=pltpu.CompilerParams(
-            has_side_effects=True, vmem_limit_bytes=16 * MIB, collective_id=5
+            has_side_effects=True, vmem_limit_bytes=42 * MIB, collective_id=5
         ),
-        name="exchange",
+        name="ladder",
     )(factors, t_local)
-
-
-def compute(right, left, t_full):
-    dma = pltpu.SemaphoreType.DMA
-    return pl.pallas_call(
-        compute_kernel,
-        out_shape=shape(32, GROUPS, 8, LANE),
-        in_specs=vmem(3),
-        out_specs=vmem(1)[0],
-        scratch_shapes=[
-            pltpu.VMEM((8, NAUX, LANE), BF16),
-            pltpu.VMEM((2 * NVP, NAUX), BF16),
-            pltpu.VMEM((2, KDIM, NVP), BF16),
-            pltpu.VMEM((4, BLOCKS, GROUPS, 8, LANE), BF16),
-            dma,
-            dma,
-        ],
-        compiler_params=pltpu.CompilerParams(
-            vmem_limit_bytes=28 * MIB, has_side_effects=True, collective_id=7
-        ),
-        name="compute",
-    )(
-        right.reshape(DEVICES, Q_LOCAL, 8, LANE),
-        left.reshape(LEFT_ROWS, DEVICES // 8, 8, LANE),
-        t_full,
-    )
 
 
 def finish(blocks):
@@ -551,7 +578,7 @@
 
 
 def on_device(factors, amplitudes):
-    return finish(compute(*exchange(factors, amplitudes)))
+    return finish(ladder(factors, amplitudes))
 
 
 def solution(mesh):

time: 127 us -> 123 us (0.969)
  Pallas kernels: 124 us -> 120 us
    pallas_call x2 -> x1, Pallas kernels: 121 us -> 117 us  [ladder(): pl.pallas_call(ladder_kernel, out_shape=shape(32, GROUPS, 8, LANE), in_sp...]
where the time goes in v4:
time: 123 us
  Pallas kernels  120 us (98%)
  local copies, waits for them, and re-layouts  2.78 us (2%)
    pallas_call x1, Pallas kernels, ladder(): pl.pallas_call(ladder_kernel, out_shape=shape(32, GROUPS, 8, LANE), in_sp...  117 us
    pallas_call x1, Pallas kernels, finish(): pl.pallas_call(finish_kernel, out_shape=shape(BLOCK, BLOCK, ROWS_X), in_s...  3.12 us
    unnamed x3, local copies, waits for them, and re-layouts  2.75 us

profile of v4, /device:TPU:1, one launch (start us, length us, event | category | flops | bytes accessed | tf_op | source)
XLA Modules:
  0.0 123.2 jit_solution(17457555247857382019)
XLA Ops:
  0.0 1.1 copy.3
  1.1 0.0 copy-start
  1.1 1.7 %copy-done = bf16[5,480,480]{2,1,0:T(8,128)(2,1)S(1)} copy-done((bf16[5,480,480]{2,1,0:T(8,128)(2,1)S(1)}, bf16[5,480,480]{2,1,0:T(8,128)(2,1)}, u32[]{:S(2)}) %copy-start) | copy-done | bytes 2304024
  2.8 117.3 %ladder.1.in_ref = bf16[32,17,8,128]{3,2,1,0:T(8,128)(2,1)S(1)} custom-call(bf16[5,480,480]{2,1,0:T(8,128)(2,1)S(1)} %copy-done, bf16[3,136,60]{2,1,0:T(8,128)(2,1)S(1)} %pad.4.t_local), custom_call_target="tpu_custom_call" | custom-call | tf_op jit(solution)/shard_map/ladder/pallas_call | solution.py:535
  120.1 3.1 %finish.1 = bf16[60,60,132]{2,1,0:T(8,128)(2,1)} custom-call(bf16[32,17,8,128]{3,2,1,0:T(8,128)(2,1)S(1)} %ladder.1.in_ref), custom_call_target="tpu_custom_call" | custom-call | tf_op jit(solution)/shard_map/finish/pallas_call | solution.py:568
  (1 shorter events, 0.0 us)
Async XLA Ops:
  1.1 1.7 %copy-start = (bf16[5,480,480]{2,1,0:T(8,128)(2,1)S(1)}, bf16[5,480,480]{2,1,0:T(8,128)(2,1)}, u32[]{:S(2)}) copy-start(bf16[5,480,480]{2,1,0:T(8,128)(2,1)} %f_ref.1) | copy-start | bytes 6912004

commit v5 on v4

--- a/solution.py
+++ b/solution.py
@@ -429,7 +429,7 @@
 
         @pl.loop(0, 4)
         def _(turn):
-            to_x = (x + turn) % 4
+            to_x = (x + 2 + turn) % 4
 
             def tiles_of(half, k, first, last):
                 return t_ref[half, k // 2, k % 2, to_x, first:last].astype(F32)

time: 123 us -> 118 us (0.959)
  Pallas kernels: 120 us -> 115 us
    pallas_call x1, Pallas kernels: 117 us -> 112 us  [ladder(): pl.pallas_call(ladder_kernel, out_shape=shape(32, GROUPS, 8, LANE), in_sp...]
where the time goes in v5:
time: 118 us; the launch traced here: 117 us
  Pallas kernels  115 us (97%)
  local copies, waits for them, and re-layouts  2.78 us (2%)
    pallas_call x1, Pallas kernels, ladder(): pl.pallas_call(ladder_kernel, out_shape=shape(32, GROUPS, 8, LANE), in_sp...  112 us
    pallas_call x1, Pallas kernels, finish(): pl.pallas_call(finish_kernel, out_shape=shape(BLOCK, BLOCK, ROWS_X), in_s...  3.13 us
    unnamed x3, local copies, waits for them, and re-layouts  2.75 us

profile of v5, /device:TPU:1, one launch (start us, length us, event | category | flops | bytes accessed | tf_op | source)
XLA Modules:
  0.0 117.5 jit_solution(11911497241464357230)
XLA Ops:
  0.0 1.1 copy.3
  1.1 0.0 copy-start
  1.1 1.7 %copy-done = bf16[5,480,480]{2,1,0:T(8,128)(2,1)S(1)} copy-done((bf16[5,480,480]{2,1,0:T(8,128)(2,1)S(1)}, bf16[5,480,480]{2,1,0:T(8,128)(2,1)}, u32[]{:S(2)}) %copy-start) | copy-done | bytes 2304024
  2.8 111.6 %ladder.1.in_ref = bf16[32,17,8,128]{3,2,1,0:T(8,128)(2,1)S(1)} custom-call(bf16[5,480,480]{2,1,0:T(8,128)(2,1)S(1)} %copy-done, bf16[3,136,60]{2,1,0:T(8,128)(2,1)S(1)} %pad.4.t_local), custom_call_target="tpu_custom_call" | custom-call | tf_op jit(solution)/shard_map/ladder/pallas_call | solution.py:535
  114.4 3.1 %finish.1 = bf16[60,60,132]{2,1,0:T(8,128)(2,1)} custom-call(bf16[32,17,8,128]{3,2,1,0:T(8,128)(2,1)S(1)} %ladder.1.in_ref), custom_call_target="tpu_custom_call" | custom-call | tf_op jit(solution)/shard_map/finish/pallas_call | solution.py:568
  (1 shorter events, 0.0 us)
Async XLA Ops:
  1.1 1.7 %copy-start = (bf16[5,480,480]{2,1,0:T(8,128)(2,1)S(1)}, bf16[5,480,480]{2,1,0:T(8,128)(2,1)}, u32[]{:S(2)}) copy-start(bf16[5,480,480]{2,1,0:T(8,128)(2,1)} %f_ref.1) | copy-start | bytes 6912004

commit v6 on v5

--- a/solution.py
+++ b/solution.py
@@ -429,7 +429,7 @@
 
         @pl.loop(0, 4)
         def _(turn):
-            to_x = (x + 2 + turn) % 4
+            to_x = (x + 2 + turn - turn // 2 * (2 * turn - 1)) % 4
 
             def tiles_of(half, k, first, last):
                 return t_ref[half, k // 2, k % 2, to_x, first:last].astype(F32)

time: 118 us -> 116 us (0.983)
  Pallas kernels: 115 us -> 113 us
    pallas_call x1, Pallas kernels: 112 us -> 110 us  [ladder(): pl.pallas_call(ladder_kernel, out_shape=shape(32, GROUPS, 8, LANE), in_sp...]
where the time goes in v6:
time: 116 us
  Pallas kernels  113 us (97%)
  local copies, waits for them, and re-layouts  2.78 us (2%)
    pallas_call x1, Pallas kernels, ladder(): pl.pallas_call(ladder_kernel, out_shape=shape(32, GROUPS, 8, LANE), in_sp...  110 us
    pallas_call x1, Pallas kernels, finish(): pl.pallas_call(finish_kernel, out_shape=shape(BLOCK, BLOCK, ROWS_X), in_s...  3.12 us
    unnamed x3, local copies, waits for them, and re-layouts  2.75 us

profile of v6, /device:TPU:1, one launch (start us, length us, event | category | flops | bytes accessed | tf_op | source)
XLA Modules:
  0.0 116.1 jit_solution(11770832927512208907)
XLA Ops:
  0.0 1.1 copy.3
  1.1 0.0 copy-start
  1.1 1.7 %copy-done = bf16[5,480,480]{2,1,0:T(8,128)(2,1)S(1)} copy-done((bf16[5,480,480]{2,1,0:T(8,128)(2,1)S(1)}, bf16[5,480,480]{2,1,0:T(8,128)(2,1)}, u32[]{:S(2)}) %copy-start) | copy-done | bytes 2304024
  2.8 110.2 %ladder.1.in_ref = bf16[32,17,8,128]{3,2,1,0:T(8,128)(2,1)S(1)} custom-call(bf16[5,480,480]{2,1,0:T(8,128)(2,1)S(1)} %copy-done, bf16[3,136,60]{2,1,0:T(8,128)(2,1)S(1)} %pad.4.t_local), custom_call_target="tpu_custom_call" | custom-call | tf_op jit(solution)/shard_map/ladder/pallas_call | solution.py:535
  113.0 3.1 %finish.1 = bf16[60,60,132]{2,1,0:T(8,128)(2,1)} custom-call(bf16[32,17,8,128]{3,2,1,0:T(8,128)(2,1)S(1)} %ladder.1.in_ref), custom_call_target="tpu_custom_call" | custom-call | tf_op jit(solution)/shard_map/finish/pallas_call | solution.py:568
  (1 shorter events, 0.0 us)
Async XLA Ops:
  1.1 1.7 %copy-start = (bf16[5,480,480]{2,1,0:T(8,128)(2,1)S(1)}, bf16[5,480,480]{2,1,0:T(8,128)(2,1)}, u32[]{:S(2)}) copy-start(bf16[5,480,480]{2,1,0:T(8,128)(2,1)} %f_ref.1) | copy-start | bytes 6912004
